TPU v7x, 32 devices: a whole 2x2x4 slice. The times are simulated.
32 devices in a mesh: brick: 8 (over z, y), pencil: 4 (over x, core).
Axes of the slice: x: 2, y: 2, z: 4, core: 2. Of those that a mesh axis runs over, the one named last changes fastest.
Arguments:
- positions: float32 [3, 131072], P(None, ('brick', 'pencil')), may hold values from 3 to 16, as said below
- charges: float32 [131072], P(('brick', 'pencil')), may hold values from -2.5 to 2.5
- anchor_row: int32 [2048], P(('brick', 'pencil')), may hold values from 0 to 115
- anchor_column: int32 [2048], P(('brick', 'pencil')), may hold values from 0 to 511
- counts: int32 [32], P(('brick', 'pencil')), may hold values from 16 to 64, as said below
Outputs:
- energy: float32 [1], replicated
- spectrum: float32 [2, 24, 512, 512], P(None, None, 'brick', 'pencil')
Inputs may be any that keep to these rules, and one draw needn't show every extreme that they name: positions[0] lies in 3 to 6, positions[1] in 3 to 16, positions[2] in 3 to 16. counts[d] is the number of live blocks of device d, the first ones of its slots; 64 is reached on some devices in every draw.
All inputs are finite; a program needn't handle non-finite values.
Results may differ from a plain program's by a relative error of at most 0.0025.
Values sent between devices are 32-bit elements; how exact they have to be, the bound alone decides.
A program may use at most 64 MiB of HBM per device.

v0:
```python
import math

import jax
import jax.numpy as jnp
from jax import lax
from jax.sharding import PartitionSpec as P

NX = 512
NY = 512
ZDEV = 3
PY = 16
PX = 16


FULL_TURN = 2.0 * math.pi
EWALD_SPLIT = 0.35
HIGHEST = lax.Precision.HIGHEST


def from_behind(block, axis, distance):
    devices = range(lax.axis_size(axis))
    route = [((i - distance) % len(devices), i) for i in devices]
    return lax.ppermute(block, axis, route)


def spline(offset):
    distance = jnp.abs(offset - 2.0)
    inner_part = (4.0 - 6.0 * distance * distance + 3.0 * distance * distance * distance) / 6.0
    remain = 2.0 - distance
    outer_part = remain * remain * remain / 6.0
    return jnp.where(distance < 1.0, inner_part, jnp.where(distance < 2.0, outer_part, 0.0))


def patches(coords, charge, patch_depth, patch_rows, patch_columns):
    blocks_here = coords.shape[1]
    atoms_here = coords.shape[2]
    weight_depth = (
        spline(coords[0][:, :, None] - jnp.arange(patch_depth, dtype=jnp.float32))
        * charge[:, :, None]
    )
    weight_rows = spline(coords[1][:, :, None] - jnp.arange(patch_rows, dtype=jnp.float32))
    weight_columns = spline(coords[2][:, :, None] - jnp.arange(patch_columns, dtype=jnp.float32))
    sheet = (weight_rows[:, :, :, None] * weight_columns[:, :, None, :]).reshape(
        blocks_here, atoms_here, patch_rows * patch_columns
    )
    return jnp.einsum("gaz,gak->gzk", weight_depth, sheet, precision=HIGHEST)


def terms_of(wave_index, length):
    signed = jnp.where(2 * wave_index >= length, wave_index - length, wave_index)
    fraction = signed.astype(jnp.float32) / length
    cosine = jnp.cos(wave_index.astype(jnp.float32) * (FULL_TURN / length))
    spline_fix = 9.0 / ((2.0 + cosine) * (2.0 + cosine))
    return (fraction * fraction, spline_fix)


def ewald_kernel(z_terms, y_terms, x_terms, length):
    squared = z_terms[0][:, None, None] + y_terms[0][None, :, None] + x_terms[0][None, None, :]
    anchor = squared == 0.0
    safe_squared = jnp.where(anchor, 1.0, squared)
    damped = jnp.exp(squared * (-(math.pi * math.pi) / (EWALD_SPLIT * EWALD_SPLIT))) / (
        safe_squared * (math.pi * (length * NY * NX))
    )
    fixes = z_terms[1][:, None, None] * y_terms[1][None, :, None] * x_terms[1][None, None, :]
    return jnp.where(anchor, 0.0, damped) * fixes


def tables(length):
    wave_index = jnp.arange(length, dtype=jnp.int32)
    phase_step = wave_index[:, None] * wave_index[None, :] % length
    angles = phase_step.astype(jnp.float32) * (FULL_TURN / length)
    return (jnp.cos(angles), jnp.sin(angles))


def transform_middle(block_data):
    cosine_table, sine_table = tables(block_data.shape[2])
    real_part = jnp.einsum(
        "ky,zyx->zkx", cosine_table, block_data[0], precision=HIGHEST
    ) + jnp.einsum("ky,zyx->zkx", sine_table, block_data[1], precision=HIGHEST)
    imag_part = jnp.einsum(
        "ky,zyx->zkx", cosine_table, block_data[1], precision=HIGHEST
    ) - jnp.einsum("ky,zyx->zkx", sine_table, block_data[0], precision=HIGHEST)
    return jnp.stack([real_part, imag_part])


def transform_leading(block_data):
    length = block_data.shape[1]
    cosine_table, sine_table = tables(length)
    flat_data = block_data.reshape(2, length, -1)
    real_part = jnp.dot(
        cosine_table, flat_data[0], precision=HIGHEST, preferred_element_type=jnp.float32
    ) + jnp.dot(sine_table, flat_data[1], precision=HIGHEST, preferred_element_type=jnp.float32)
    imag_part = jnp.dot(
        cosine_table, flat_data[1], precision=HIGHEST, preferred_element_type=jnp.float32
    ) - jnp.dot(sine_table, flat_data[0], precision=HIGHEST, preferred_element_type=jnp.float32)
    return jnp.stack([real_part, imag_part]).reshape(block_data.shape)


def spread_into(
    coords,
    charge,
    anchor_row,
    anchor_column,
    padded_rows,
    columns,
    patch_depth,
    group_size,
    turn_count,
):
    row_cells = jnp.arange(padded_rows, dtype=jnp.int32)
    column_cells = jnp.arange(columns, dtype=jnp.int32)
    line_steps = jnp.arange(PY, dtype=jnp.int32)
    cell_steps = jnp.arange(PX, dtype=jnp.int32)

    def one_group(turn_index, accumulated):
        first_slot = turn_index * group_size
        part_coords = lax.dynamic_slice_in_dim(coords, first_slot, group_size, 1)
        part_charge = lax.dynamic_slice_in_dim(charge, first_slot, group_size, 0)
        part_rows = lax.dynamic_slice_in_dim(anchor_row, first_slot, group_size, 0)
        part_columns = lax.dynamic_slice_in_dim(anchor_column, first_slot, group_size, 0)
        values = patches(part_coords, part_charge, patch_depth, PY, PX).reshape(
            group_size, patch_depth, PY, PX
        )
        column_place = (
            ((part_columns[:, None] + cell_steps[None, :]) % columns)[:, :, None]
            == column_cells[None, None, :]
        ).astype(jnp.float32)
        row_place = (
            (part_rows[:, None] + line_steps[None, :])[:, :, None] == row_cells[None, None, :]
        ).astype(jnp.float32)
        placed_columns = jnp.einsum("gjlm,gmx->gjlx", values, column_place, precision=HIGHEST)
        return accumulated + jnp.einsum(
            "gjlx,glr->jrx", placed_columns, row_place, precision=HIGHEST
        )

    return lax.fori_loop(
        0, turn_count, one_group, jnp.zeros((patch_depth, padded_rows, columns), jnp.float32)
    )


def shards(positions, charges, anchor_row, anchor_column, counts):
    slot_count = anchor_row.shape[0]
    block_atoms = charges.shape[0] // slot_count
    pencil_rows = NY // lax.axis_size("pencil")
    patch_depth = ZDEV + 3
    padded_rows = pencil_rows + 3
    group_size = math.gcd(slot_count, 16)
    coords = positions.reshape(3, slot_count, block_atoms)
    live_mask = (jnp.arange(slot_count, dtype=jnp.int32) < counts[0]).astype(jnp.float32)
    charge = charges.reshape(slot_count, block_atoms) * live_mask[:, None]
    turn_count = slot_count // group_size
    local_grid = spread_into(
        coords,
        charge,
        anchor_row,
        anchor_column,
        padded_rows,
        NX,
        patch_depth,
        group_size,
        turn_count,
    )
    received = from_behind(local_grid[:3], "brick", -1)
    upper_planes = local_grid[3:]
    slab_grid = jnp.concatenate([upper_planes[: ZDEV - 3], upper_planes + received], axis=0)
    row_rim = from_behind(slab_grid[:, :3], "pencil", -1)
    inner_rows = slab_grid[:, 3:]
    charge_grid = jnp.concatenate(
        [inner_rows[:, : pencil_rows - 3], inner_rows[:, pencil_rows - 3 :] + row_rim], axis=1
    )
    cosine_table, sine_table = tables(NX)
    flat_rows = charge_grid.reshape(ZDEV * pencil_rows, NX)
    real_part = jnp.dot(
        flat_rows, cosine_table, precision=HIGHEST, preferred_element_type=jnp.float32
    )
    imag_part = -jnp.dot(
        flat_rows, sine_table, precision=HIGHEST, preferred_element_type=jnp.float32
    )
    after_x = jnp.stack([real_part, imag_part]).reshape(2, ZDEV, pencil_rows, NX)
    after_y = transform_middle(
        lax.all_to_all(after_x, "pencil", split_axis=3, concat_axis=2, tiled=True)
    )
    transformed = transform_leading(
        lax.all_to_all(after_y, "brick", split_axis=2, concat_axis=1, tiled=True)
    )
    length = transformed.shape[1]
    row_part = transformed.shape[2]
    column_part = transformed.shape[3]
    wave_depth = jnp.arange(length, dtype=jnp.int32)
    wave_rows = lax.axis_index("brick") * row_part + jnp.arange(row_part, dtype=jnp.int32)
    wave_columns = lax.axis_index("pencil") * column_part + jnp.arange(column_part, dtype=jnp.int32)
    kernel = ewald_kernel(
        terms_of(wave_depth, length), terms_of(wave_rows, NY), terms_of(wave_columns, NX), length
    )
    power = transformed[0] * transformed[0] + transformed[1] * transformed[1]
    local_energy = jnp.sum(kernel * power)
    total_energy = lax.psum(local_energy, ("brick", "pencil"))
    slot_total = slot_count * lax.axis_size("brick") * lax.axis_size("pencil")
    energy = (total_energy * (0.5 / slot_total)).reshape(1)
    return (energy, transformed)


def solution(mesh):
    return jax.shard_map(
        shards,
        mesh=mesh,
        in_specs=(
            P(None, ("brick", "pencil")),
            P(("brick", "pencil")),
            P(("brick", "pencil")),
            P(("brick", "pencil")),
            P(("brick", "pencil")),
        ),
        out_specs=(P(), P(None, None, "brick", "pencil")),
        check_vma=False,
    )
```

profile of v0, /device:TPU:0, one launch (start us, length us, event | category | flops | bytes accessed | tf_op | source)
XLA Modules:
  0.0 225.5 jit_solution(9874964305183210134)
XLA Ops:
  3.1 40.4 %while.18 = (s32[]{:T(128)}, f32[6,131,512]{2,1,0:T(8,128)}, s32[64]{0:T(128)}, f32[3,64,64]{2,1,0:T(8,128)S(1)}, f32[64,64]{1,0:T(8,128)S(1)}, /*index=5*/s32[6...) while((s32[]{:T(128)}, f32[6,131,512]{2,1,0:T(8,128)}, ...), condition=%wide.region_1.2_spmd.clone.clone, body=%wide.region_0.1_spmd.clone.clone.sunk | while | flops 1408120832 | bytes 12515989 | solution.py:136
  3.6 1.8 fusion.193
  6.7 2.6 %fusion.194 = f32[16,6,16,512]{3,2,0,1:T(8,128)S(1)} fusion(f32[16,6,16,16]{3,2,0,1:T(8,128)} %reshape.343, s32[16,16]{1,0:T(8,128)S(1)} %add_select_fusion.4), kind=kOutput, calls=%fused_computation.7.clone.1 | convolution fusion | flops 151126016 | bytes 3245056 | tf_op jit(solution)/shard_map/while/body/eval_jaxpr/gjlm,gmx->gjlx/dot_general | solution.py:131
  9.4 2.7 %bitcast_add_fusion.3 = f32[6,131,512]{2,1,0:T(8,128)} fusion(f32[6,131,512]{2,1,0:T(8,128)} %get-tuple-element.429, f32[16,6,16,512]{3,2,0,1:T(8,128)S(1)} %fusion.194, pred[]{:T(512)S(6)} %compare.6, s32[16,16]{1,0:T(8,128)S(1)} %iota_add_fusion.6), kind=kOutput, calls=%fused_computation.3.clone.1 | convolution fusion | flops 1237109504 | bytes 6366209 | tf_op jit(solution)/shard_map/while/body/eval_jaxpr/gjlx,glr->jrx/dot_general | solution.py:132
  12.6 1.8 fusion.193
  15.7 2.6 %fusion.194 = f32[16,6,16,512]{3,2,0,1:T(8,128)S(1)} fusion(f32[16,6,16,16]{3,2,0,1:T(8,128)} %reshape.343, s32[16,16]{1,0:T(8,128)S(1)} %add_select_fusion.4), kind=kOutput, calls=%fused_computation.7.clone.1 | convolution fusion | flops 151126016 | bytes 3245056 | tf_op jit(solution)/shard_map/while/body/eval_jaxpr/gjlm,gmx->gjlx/dot_general | solution.py:131
  18.4 4.2 %bitcast_add_fusion.3 = f32[6,131,512]{2,1,0:T(8,128)} fusion(f32[6,131,512]{2,1,0:T(8,128)} %get-tuple-element.429, f32[16,6,16,512]{3,2,0,1:T(8,128)S(1)} %fusion.194, pred[]{:T(512)S(6)} %compare.6, s32[16,16]{1,0:T(8,128)S(1)} %iota_add_fusion.6), kind=kOutput, calls=%fused_computation.3.clone.1 | convolution fusion | flops 1237109504 | bytes 6366209 | tf_op jit(solution)/shard_map/while/body/eval_jaxpr/gjlx,glr->jrx/dot_general | solution.py:132
  23.0 1.8 fusion.193
  26.2 2.6 %fusion.194 = f32[16,6,16,512]{3,2,0,1:T(8,128)S(1)} fusion(f32[16,6,16,16]{3,2,0,1:T(8,128)} %reshape.343, s32[16,16]{1,0:T(8,128)S(1)} %add_select_fusion.4), kind=kOutput, calls=%fused_computation.7.clone.1 | convolution fusion | flops 151126016 | bytes 3245056 | tf_op jit(solution)/shard_map/while/body/eval_jaxpr/gjlm,gmx->gjlx/dot_general | solution.py:131
  28.9 4.2 %bitcast_add_fusion.3 = f32[6,131,512]{2,1,0:T(8,128)} fusion(f32[6,131,512]{2,1,0:T(8,128)} %get-tuple-element.429, f32[16,6,16,512]{3,2,0,1:T(8,128)S(1)} %fusion.194, pred[]{:T(512)S(6)} %compare.6, s32[16,16]{1,0:T(8,128)S(1)} %iota_add_fusion.6), kind=kOutput, calls=%fused_computation.3.clone.1 | convolution fusion | flops 1237109504 | bytes 6366209 | tf_op jit(solution)/shard_map/while/body/eval_jaxpr/gjlx,glr->jrx/dot_general | solution.py:132
  33.5 1.8 fusion.193
  36.6 2.6 %fusion.194 = f32[16,6,16,512]{3,2,0,1:T(8,128)S(1)} fusion(f32[16,6,16,16]{3,2,0,1:T(8,128)} %reshape.343, s32[16,16]{1,0:T(8,128)S(1)} %add_select_fusion.4), kind=kOutput, calls=%fused_computation.7.clone.1 | convolution fusion | flops 151126016 | bytes 3245056 | tf_op jit(solution)/shard_map/while/body/eval_jaxpr/gjlm,gmx->gjlx/dot_general | solution.py:131
  39.4 4.2 %bitcast_add_fusion.3 = f32[6,131,512]{2,1,0:T(8,128)} fusion(f32[6,131,512]{2,1,0:T(8,128)} %get-tuple-element.429, f32[16,6,16,512]{3,2,0,1:T(8,128)S(1)} %fusion.194, pred[]{:T(512)S(6)} %compare.6, s32[16,16]{1,0:T(8,128)S(1)} %iota_add_fusion.6), kind=kOutput, calls=%fused_computation.3.clone.1 | convolution fusion | flops 1237109504 | bytes 6366209 | tf_op jit(solution)/shard_map/while/body/eval_jaxpr/gjlx,glr->jrx/dot_general | solution.py:132
  43.5 1.3 slice.75
  44.9 6.1 %collective-permute-start = (f32[3,131,512]{2,1,0:T(8,128)S(1)}, f32[3,131,512]{2,1,0:T(8,128)S(1)}, u32[]{:S(2)}, u32[]{:S(2)}) collective-permute-start(f32[3,131,512]{2,1,0:T(8,128)S(1)} %slice.75), channel_id=1, source_target_pairs={{4,0},{8,4},{12,8},{16,12},{20,16},{24,20},{28,24},{0,28},{5,1},{9... | collective-permute-start | bytes 2414600 | tf_op jit(solution)/shard_map/ppermute | solution.py:23
  50.9 17.9 %collective-permute-done = f32[3,131,512]{2,1,0:T(8,128)S(1)} collective-permute-done((f32[3,131,512]{2,1,0:T(8,128)S(1)}, f32[3,131,512]{2,1,0:T(8,128)S(1)}, u32[]{:S(2)}, u32[]{:S(2)}) %collective-permute-start) | collective-permute-done | bytes 804896 | tf_op jit(solution)/shard_map/ppermute | solution.py:23
  69.3 1.4 collective-permute-done.1
  70.8 5.8 %convolution_bitcast_fusion = f32[1,3,128,512]{3,2,1,0:T(8,128)S(1)} fusion(f32[3,128,512]{2,1,0:T(8,128)S(1)} %pad_maximum_fusion.3), kind=kOutput, calls=%fused_computation.95 | convolution fusion | flops 1211629568 | bytes 1572864 | tf_op jit(solution)/shard_map/dot_general | solution.py:173
  76.6 5.7 %convolution_negate_fusion = f32[384,512]{1,0:T(8,128)S(1)} fusion(f32[384,512]{1,0:T(8,128)S(1)} %bitcast.137), kind=kOutput, calls=%fused_computation.94 | convolution fusion | flops 1211826176 | bytes 1572864 | tf_op jit(solution)/shard_map/dot_general | solution.py:176
  83.8 22.9 %all_to_all.30 = f32[2,3,128,512]{2,0,1,3:T(2,128)S(1)} all-to-all(f32[2,3,128,512]{2,0,1,3:T(2,128)S(1)} %copy.26), channel_id=1, replica_groups=mesh['brick'=8,'pencil'=4] {'pencil'}, dimensions={3} | all-to-all | bytes 3145728 | tf_op jit(solution)/shard_map/all_to_all | solution.py:181
  108.1 5.8 %fusion.75 = f32[3,128,512]{2,1,0:T(8,128)S(1)} fusion(f32[3,512,128]{1,2,0:T(8,128)S(1)} %squeeze.17), kind=kOutput, calls=%fused_computation.103 | convolution fusion | flops 1211629568 | bytes 1572864 | tf_op jit(solution)/shard_map/ky,zyx->zkx/dot_general | solution.py:77
  114.3 5.8 %fusion.73 = f32[3,128,512]{2,1,0:T(8,128)S(1)} fusion(f32[3,512,128]{1,2,0:T(8,128)S(1)} %squeeze.18), kind=kOutput, calls=%fused_computation.101 | convolution fusion | flops 1211629568 | bytes 1572864 | tf_op jit(solution)/shard_map/ky,zyx->zkx/dot_general | solution.py:80
  120.1 5.8 %fusion.66 = f32[1,3,512,128]{2,3,1,0:T(8,128)S(1)} fusion(f32[3,128,512]{2,1,0:T(8,128)S(1)} %fusion.75, f32[3,512,128]{1,2,0:T(8,128)S(1)} %squeeze.18), kind=kOutput, calls=%fused_computation.92 | convolution fusion | flops 1211826176 | bytes 2359296 | tf_op jit(solution)/shard_map/ky,zyx->zkx/dot_general | solution.py:79
  125.9 6.1 %fusion.67 = f32[1,3,512,128]{2,3,1,0:T(8,128)S(1)} fusion(f32[3,128,512]{2,1,0:T(8,128)S(1)} %fusion.73, f32[3,512,128]{1,2,0:T(8,128)S(1)} %squeeze.17), kind=kOutput, calls=%fused_computation.93 | convolution fusion | flops 1211826176 | bytes 2359296 | tf_op jit(solution)/shard_map/ky,zyx->zkx/dot_general | solution.py:82
  132.2 2.1 copy.28
  134.3 6.5 %all-to-all-start.1 = ((f32[2,3,512,128]{3,0,1,2:T(2,128)}), f32[2,3,512,128]{3,0,1,2:T(2,128)S(1)}, u32[]{:S(2)}, u32[]{:S(2)}) async-start(f32[2,3,512,128]{3,0,1,2:T(2,128)} %copy.28), calls=%async_computation.1 | async-start | bytes 3145728 | tf_op jit(solution)/shard_map/all_to_all | solution.py:184
  141.1 36.3 %all-to-all-done.1 = f32[2,3,512,128]{3,0,1,2:T(2,128)S(1)} async-done(((f32[2,3,512,128]{3,0,1,2:T(2,128)}), f32[2,3,512,128]{3,0,1,2:T(2,128)S(1)}, u32[]{:S(2)}, u32[]{:S(2)}) %all-to-all-start.1) | async-done | bytes 1572896 | tf_op jit(solution)/shard_map/all_to_all | solution.py:184
  177.8 1.2 fusion.89
  179.0 1.2 fusion.85
  182.0 2.8 %fusion.91 = (f32[]{:T(128)}, f32[24,8192]{1,0:T(8,128)S(1)}) fusion(f32[24,8192]{1,0:T(8,128)S(1)} %convolution_add_fusion, f32[3,8,64,128]{3,2,1,0:T(8,128)S(1)} %bitcast.135, f32[3,8,64,128]{3,2,1,0:T(8,128)S(1)} %bitcast.134, f32[8192]{0:T(1024)S(1)} %broadcast_bitcast_fusion, f32[8192]{0:T(1024)S(1)} %broadcast_bitcast_fusion.1, ...), kind=kOutput, calls=%fused_computation.125 | convolution fusion | flops 59577408 | bytes 4784132 | tf_op jit(solution)/shard_map/dot_general | solution.py:95
  185.1 37.5 %psum.7 = f32[]{:T(128)} all-reduce(f32[]{:T(128)} %get-tuple-element.363), channel_id=1, replica_groups=mesh['brick'=8,'pencil'=4] {'brick','pencil'}, use_global_device_ids=true, to_apply=%region_3.4 | all-reduce | flops 1 | bytes 8 | tf_op jit(solution)/shard_map/psum | solution.py:197
  222.5 1.2 pad_maximum_fusion.2
  (93 shorter events, 16.1 us)
Async XLA Ops:
  3.5 3.0 %copy-start.2 = (s32[64]{0:T(128)S(1)}, s32[64]{0:T(128)}, u32[]{:S(2)}) copy-start(s32[64]{0:T(128)} %get-tuple-element.445) | copy-start | bytes 772 | tf_op jit(solution)/shard_map/while
  6.7 2.6 %copy-start.1 = (s32[64]{0:T(128)S(1)}, s32[64]{0:T(128)}, u32[]{:S(2)}) copy-start(s32[64]{0:T(128)} %get-tuple-element.442) | copy-start | bytes 772 | tf_op jit(solution)/shard_map/while
  12.6 3.0 %copy-start.2 = (s32[64]{0:T(128)S(1)}, s32[64]{0:T(128)}, u32[]{:S(2)}) copy-start(s32[64]{0:T(128)} %get-tuple-element.445) | copy-start | bytes 772 | tf_op jit(solution)/shard_map/while
  15.7 2.6 %copy-start.1 = (s32[64]{0:T(128)S(1)}, s32[64]{0:T(128)}, u32[]{:S(2)}) copy-start(s32[64]{0:T(128)} %get-tuple-element.442) | copy-start | bytes 772 | tf_op jit(solution)/shard_map/while
  23.0 3.0 %copy-start.2 = (s32[64]{0:T(128)S(1)}, s32[64]{0:T(128)}, u32[]{:S(2)}) copy-start(s32[64]{0:T(128)} %get-tuple-element.445) | copy-start | bytes 772 | tf_op jit(solution)/shard_map/while
  26.1 2.6 %copy-start.1 = (s32[64]{0:T(128)S(1)}, s32[64]{0:T(128)}, u32[]{:S(2)}) copy-start(s32[64]{0:T(128)} %get-tuple-element.442) | copy-start | bytes 772 | tf_op jit(solution)/shard_map/while
  33.5 3.0 %copy-start.2 = (s32[64]{0:T(128)S(1)}, s32[64]{0:T(128)}, u32[]{:S(2)}) copy-start(s32[64]{0:T(128)} %get-tuple-element.445) | copy-start | bytes 772 | tf_op jit(solution)/shard_map/while
  36.6 2.6 %copy-start.1 = (s32[64]{0:T(128)S(1)}, s32[64]{0:T(128)}, u32[]{:S(2)}) copy-start(s32[64]{0:T(128)} %get-tuple-element.442) | copy-start | bytes 772 | tf_op jit(solution)/shard_map/while
  43.5 25.2 %copy-start = (f32[6,131,512]{2,1,0:T(8,128)S(1)}, f32[6,131,512]{2,1,0:T(8,128)}, u32[]{:S(2)}) copy-start(f32[6,131,512]{2,1,0:T(8,128)} %get-tuple-element.292) | copy-start | bytes 4829188
  44.9 23.9 %collective-permute-start = (f32[3,131,512]{2,1,0:T(8,128)S(1)}, f32[3,131,512]{2,1,0:T(8,128)S(1)}, u32[]{:S(2)}, u32[]{:S(2)}) collective-permute-start(f32[3,131,512]{2,1,0:T(8,128)S(1)} %slice.75), channel_id=1, source_target_pairs={{4,0},{8,4},{12,8},{16,12},{20,16},{24,20},{28,24},{0,28},{5,1},{9... | collective-permute-start | bytes 2414600 | tf_op jit(solution)/shard_map/ppermute | solution.py:23
  68.9 1.8 collective-permute-start.1
  134.3 43.1 %all-to-all-start.1 = ((f32[2,3,512,128]{3,0,1,2:T(2,128)}), f32[2,3,512,128]{3,0,1,2:T(2,128)S(1)}, u32[]{:S(2)}, u32[]{:S(2)}) async-start(f32[2,3,512,128]{3,0,1,2:T(2,128)} %copy.28), calls=%async_computation.1 | async-start | bytes 3145728 | tf_op jit(solution)/shard_map/all_to_all | solution.py:184
where the time goes:
time: 227 us; the launch traced here: 226 us
  matrix products  74 us (33%)
  blocking collectives  60.4 us (27%)
  waiting for transfers between devices  55.6 us (24%)
  local copies, waits for them, and re-layouts  14.8 us (7%)
  starting transfers between devices  12.8 us (6%)
  other arithmetic  4.4 us (2%)
  between operations  3.3 us (1%)
    psum x1, blocking collectives, shards(): total_energy = lax.psum(local_energy, ('brick', 'pencil'))  37.5 us
    all_to_all x1, waiting for transfers between devices, shards(): lax.all_to_all(after_y, 'brick', split_axis=2, concat_axis=1, tiled=True)  36.3 us
    all_to_all x1, blocking collectives, shards(): lax.all_to_all(after_x, 'pencil', split_axis=3, concat_axis=2, tiled=True)  22.9 us
    ppermute x2, waiting for transfers between devices, from_behind(): return lax.ppermute(block, axis, route)  19.3 us
    dot_general x4, matrix products, one_group(): jnp.einsum('gjlx,glr->jrx', placed_columns, row_place, precision=HIGHEST)  15.2 us
    dot_general x4, matrix products, one_group(): jnp.einsum('gjlm,gmx->gjlx', values, column_place, precision=HIGHEST)  10.3 us
    dot_general x4, matrix products, patches(): return jnp.einsum('gaz,gak->gzk', weight_depth, sheet, precision=HIGHEST)  7.03 us
    all_to_all x1, starting transfers between devices, shards(): lax.all_to_all(after_y, 'brick', split_axis=2, concat_axis=1, tiled=True)  6.45 us
  transfers between devices with their start and end apart: 3, of which 3 were waited for; matrix products, arithmetic and copies ran while one was open for 0% of the time, Pallas kernels for 0%

commit v1 on v0

v1 whole, which is shorter than its diff:
```python
import functools
import math

import jax
import jax.numpy as jnp
import numpy as np
from jax import lax
from jax.experimental import pallas as pl
from jax.experimental.pallas import tpu as pltpu
from jax.sharding import PartitionSpec as P

NX = 512
NY = 512
ZDEV = 3
PY = 16
PX = 16
LANES = 128
RIM = 8
GROUP = 4

FULL_TURN = 2.0 * math.pi
EWALD_SPLIT = 0.35
HIGH = lax.Precision.HIGH


def from_behind(block, axis, distance):
    devices = range(lax.axis_size(axis))
    route = [((i - distance) % len(devices), i) for i in devices]
    return lax.ppermute(block, axis, route)


def spline(offset):
    distance = jnp.abs(offset - 2.0)
    outer = jnp.maximum(2.0 - distance, 0.0)
    inner = jnp.maximum(1.0 - distance, 0.0)
    return (outer * outer * outer - 4.0 * (inner * inner * inner)) * (1.0 / 6.0)


def split(value):
    high = value.astype(jnp.bfloat16)
    low = (value - high.astype(jnp.float32)).astype(jnp.bfloat16)
    return high, low


def dot3(left, right, dims):
    def one(a, b):
        return lax.dot_general(a, b, (dims, ((), ())), preferred_element_type=jnp.float32)

    return one(left[0], right[1]) + one(left[1], right[0]) + one(left[0], right[0])


def spread_kernel(first_plane, block_atoms, *refs):
    row_ref, column_ref, coords_ref, charge_ref, *before, grid_ref = refs
    slots = row_ref.shape[0]
    if before:
        grid_ref[...] = before[0][...]
    else:
        grid_ref[...] = jnp.zeros_like(grid_ref)
    tiles = grid_ref.shape[0]
    width = GROUP * block_atoms
    lane_block = lax.broadcasted_iota(jnp.int32, (PY, width), 1) // block_atoms
    steps = lax.broadcasted_iota(jnp.int32, (PY, width), 0).astype(jnp.float32)
    planes = (lax.broadcasted_iota(jnp.int32, (8, width), 0) + first_plane).astype(jnp.float32)
    lane = lax.broadcasted_iota(jnp.int32, (ZDEV * PY, LANES), 1)
    blank = jnp.zeros((LANES - PX, width), jnp.bfloat16)

    def turn(step, carry):
        here = pl.ds(pl.multiple_of(step * width, width), width)
        depth = spline(coords_ref[0:1, here] - planes) * charge_ref[0:1, here]
        lines = spline(coords_ref[1:2, here] - steps)
        cells = split(spline(coords_ref[2:3, here] - steps))
        cells = [jnp.concatenate([part, blank], axis=0) for part in cells]
        pieces = []
        for member in range(GROUP):
            own = jnp.where(lane_block == member, lines, 0.0)
            for plane in range(ZDEV):
                pieces.append(split(own * depth[plane : plane + 1]))
        sheets = [jnp.concatenate([piece[i] for piece in pieces], axis=0) for i in range(2)]
        values = dot3(sheets, cells, ((1,), (1,)))
        for member in range(GROUP):
            block = step * GROUP + member
            column = column_ref[block]
            row = row_ref[block] + (RIM - 3)
            shift = column & (LANES - 1)
            tile = column // LANES
            over = (tile + 1) & (tiles - 1)
            patch = values[member * ZDEV * PY : (member + 1) * ZDEV * PY]
            patch = pltpu.roll(patch, shift, 1)
            parts = (
                (tile, jnp.where(lane >= shift, patch, 0.0)),
                (over, jnp.where(lane >= shift, 0.0, patch)),
            )
            sums = []
            for where, part in parts:
                for plane in range(ZDEV):
                    old = grid_ref[where, plane, pl.ds(row, PY), :]
                    sums.append(old + part[plane * PY : (plane + 1) * PY])
            for index, (where, part) in enumerate(parts):
                for plane in range(ZDEV):
                    grid_ref[where, plane, pl.ds(row, PY), :] = sums[index * ZDEV + plane]
        return carry

    lax.fori_loop(0, slots // GROUP, turn, 0)


def spread(first_plane, rows, anchor_row, anchor_column, coords, charge, *before):
    slots = anchor_row.shape[0]
    shape = (NX // LANES, ZDEV, rows + RIM, LANES)
    scalar = pl.BlockSpec(memory_space=pltpu.SMEM)
    whole = pl.BlockSpec(memory_space=pltpu.VMEM)
    return pl.pallas_call(
        functools.partial(spread_kernel, first_plane, charge.shape[1] // slots),
        out_shape=jax.ShapeDtypeStruct(shape, jnp.float32),
        in_specs=[scalar, scalar] + [whole] * (2 + len(before)),
        out_specs=whole,
        compiler_params=pltpu.CompilerParams(vmem_limit_bytes=24 * 1024 * 1024),
        cost_estimate=pl.CostEstimate(
            flops=20_000_000, bytes_accessed=4_000_000, transcendentals=0
        ),
    )(anchor_row, anchor_column, coords, charge, *before)


def terms_of(wave_index, length):
    signed = jnp.where(2 * wave_index >= length, wave_index - length, wave_index)
    fraction = signed.astype(jnp.float32) / length
    cosine = jnp.cos(wave_index.astype(jnp.float32) * (FULL_TURN / length))
    spline_fix = 9.0 / ((2.0 + cosine) * (2.0 + cosine))
    return (fraction * fraction, spline_fix)


def ewald_kernel(z_terms, y_terms, x_terms, length):
    squared = z_terms[0][:, None, None] + y_terms[0][None, :, None] + x_terms[0][None, None, :]
    anchor = squared == 0.0
    safe_squared = jnp.where(anchor, 1.0, squared)
    damped = jnp.exp(squared * (-(math.pi * math.pi) / (EWALD_SPLIT * EWALD_SPLIT))) / (
        safe_squared * (math.pi * (length * NY * NX))
    )
    fixes = z_terms[1][:, None, None] * y_terms[1][None, :, None] * x_terms[1][None, None, :]
    return jnp.where(anchor, 0.0, damped) * fixes


def tables(length):
    steps = np.arange(length)
    angles = (steps[:, None] * steps[None, :] % length) * (FULL_TURN / length)
    return np.cos(angles).astype(np.float32), np.sin(angles).astype(np.float32)


def transform_by_steps(grid, rows):
    pencils = lax.axis_size("pencil")
    tiles, _, _, _ = grid.shape
    cosine, sine = tables(NX)
    both = np.stack([cosine, -sine], axis=1).reshape(tiles, LANES, 2, NX)
    after_x = jnp.einsum("tzrl,tlck->czrk", grid, both, precision=HIGH)
    got = lax.all_to_all(after_x[:, None], "pencil", split_axis=4, concat_axis=1, tiled=True)
    rim = jnp.roll(got[:, :, :, :RIM], -1, axis=1)
    body = got[:, :, :, RIM:]
    body = jnp.concatenate([body[:, :, :, : rows - RIM], body[:, :, :, rows - RIM :] + rim], axis=3)
    cosine, sine = tables(NY)
    shape = (pencils, rows, NY)
    turn = np.stack([np.stack([cosine, sine]), np.stack([-sine, cosine])])
    turn = turn.reshape(2, 2, *shape)
    after_y = jnp.einsum("dcprk,cpzrx->dzkx", turn, body, precision=HIGH)
    got = lax.all_to_all(after_y, "brick", split_axis=2, concat_axis=1, tiled=True)
    length = got.shape[1]
    cosine, sine = tables(length)
    turn = np.stack([np.stack([cosine, sine]), np.stack([-sine, cosine])])
    transformed = jnp.einsum("dczk,czyx->dkyx", turn, got, precision=HIGH)
    row_part = transformed.shape[2]
    column_part = transformed.shape[3]
    wave_depth = jnp.arange(length, dtype=jnp.int32)
    wave_rows = lax.axis_index("brick") * row_part + jnp.arange(row_part, dtype=jnp.int32)
    wave_columns = lax.axis_index("pencil") * column_part + jnp.arange(column_part, dtype=jnp.int32)
    kernel = ewald_kernel(
        terms_of(wave_depth, length), terms_of(wave_rows, NY), terms_of(wave_columns, NX), length
    )
    power = transformed[0] * transformed[0] + transformed[1] * transformed[1]
    total = lax.psum(jnp.sum(kernel * power), ("brick", "pencil"))
    return total.reshape(1), transformed


def shards(positions, charges, anchor_row, anchor_column, counts):
    slot_count = anchor_row.shape[0]
    atoms = charges.shape[0]
    block_atoms = atoms // slot_count
    rows = NY // lax.axis_size("pencil")
    live = jnp.arange(atoms, dtype=jnp.int32) < counts[0] * block_atoms
    charge = (charges * live.astype(jnp.float32)).reshape(1, atoms)
    other = [
        from_behind(array, "brick", -1) for array in (anchor_row, anchor_column, positions, charge)
    ]
    grid = spread(3, rows, anchor_row, anchor_column, positions, charge)
    grid = spread(0, rows, *other, grid)
    total, spectrum = transform_by_steps(grid, rows)
    slot_total = slot_count * lax.axis_size("brick") * lax.axis_size("pencil")
    return (total * (0.5 / slot_total), spectrum)


def solution(mesh):
    return jax.shard_map(
        shards,
        mesh=mesh,
        in_specs=(
            P(None, ("brick", "pencil")),
            P(("brick", "pencil")),
            P(("brick", "pencil")),
            P(("brick", "pencil")),
            P(("brick", "pencil")),
        ),
        out_specs=(P(), P(None, None, "brick", "pencil")),
        check_vma=False,
    )
```

time: 227 us -> 164 us (0.72)
  matrix products: 74 us -> 7.62 us
  waiting for transfers between devices: 55.6 us -> 36.3 us
  blocking collectives: 60.4 us -> 76.8 us
  Pallas kernels: 0 us -> 10.9 us
    dot_general x22 -> x3, matrix products: 74 us -> 7.62 us  [the longest x1 3.06 us: transform_by_steps(): after_y = jnp.einsum('dcprk,cpzrx->dzkx', turn, body, precision=HIGH)]
    ppermute x2 -> x4, waiting for transfers between devices: 19.3 us -> 0.01 us  [from_behind(): return lax.ppermute(block, axis, route)]
    all_to_all x1, blocking collectives: 22.9 us -> 39.5 us  [transform_by_steps(): lax.all_to_all(after_x[:, None], 'pencil', split_axis=4, concat_axis=1, t...]
    pallas_call x0 -> x2, Pallas kernels: none -> 10.9 us  [spread(): pl.pallas_call(functools.partial(spread_kernel, first_plane, charge.shape...]
    reshape x6 -> x0, local copies, waits for them, and re-layouts: 6.31 us -> none  [the longest x4 4.56 us: one_group(): patches(part_coords, part_charge, patch_depth, PY, PX)]
    unnamed x4 -> x13, local copies, waits for them, and re-layouts: 0.28 us -> 6.13 us
    broadcast_in_dim x0 -> x1, local copies, waits for them, and re-layouts: none -> 3.99 us  [transform_by_steps(): after_x[:, None]]
    another operation x2 -> x0, local copies, waits for them, and re-layouts: 3.24 us -> none  [the longest x1 2.08 us: transform_middle(): return jnp.stack([real_part, imag_part])]
  transfers between devices with their start and end apart: 3 -> 5, of which waited for: 3 -> 1; matrix products, arithmetic and copies ran while one was open for 0% -> 1% of each run, Pallas kernels for 0% -> 3%
where the time goes in v1:
time: 164 us; the launch traced here: 163 us
  blocking collectives  76.8 us (47%)
  waiting for transfers between devices  36.3 us (22%)
  local copies, waits for them, and re-layouts  13.4 us (8%)
  starting transfers between devices  12.3 us (8%)
  Pallas kernels  10.9 us (7%)
  matrix products  7.62 us (5%)
  between operations  3.22 us (2%)
  other arithmetic  2.38 us (1%)
    all_to_all x1, blocking collectives, transform_by_steps(): lax.all_to_all(after_x[:, None], 'pencil', split_axis=4, concat_axis=1, t...  39.5 us
    psum x1, blocking collectives, transform_by_steps(): total = lax.psum(jnp.sum(kernel * power), ('brick', 'pencil'))  37.3 us
    all_to_all x1, waiting for transfers between devices, transform_by_steps(): lax.all_to_all(after_y, 'brick', split_axis=2, concat_axis=1, tiled=True)  36.3 us
    pallas_call x2, Pallas kernels, spread(): pl.pallas_call(functools.partial(spread_kernel, first_plane, charge.shape...  10.9 us
    ppermute x4, starting transfers between devices, from_behind(): return lax.ppermute(block, axis, route)  8.48 us
    unnamed x13, local copies, waits for them, and re-layouts  6.13 us
    broadcast_in_dim x1, local copies, waits for them, and re-layouts, transform_by_steps(): after_x[:, None]  3.99 us
    all_to_all x1, starting transfers between devices, transform_by_steps(): lax.all_to_all(after_y, 'brick', split_axis=2, concat_axis=1, tiled=True)  3.8 us
  transfers between devices with their start and end apart: 5, of which 1 were waited for; matrix products, arithmetic and copies ran while one was open for 1% of the time, Pallas kernels for 3%

profile of v1, /device:TPU:0, one launch (start us, length us, event | category | flops | bytes accessed | tf_op | source)
XLA Modules:
  0.0 162.9 jit_solution(14486603720075777076)
XLA Ops:
  0.6 6.1 %collective-permute-start.2 = (f32[3,4096]{1,0:T(4,128)}, f32[3,4096]{1,0:T(4,128)S(1)}, u32[]{:S(2)}, u32[]{:S(2)}) collective-permute-start(f32[3,4096]{1,0:T(4,128)} %refs_2_.1), channel_id=1, source_target_pairs={{4,0},{8,4},{12,8},{16,12},{20,16},{24,20},{28,24},{0,28},{5,1},{9... | collective-permute-start | bytes 147464 | tf_op jit(solution)/shard_map/ppermute | solution.py:29
  7.3 0.7 fusion.20
  8.1 0.5 collective-permute-start.3
  8.6 1.4 collective-permute-start
  10.0 0.5 collective-permute-start.1
  10.5 0.8 copy-done
  11.3 0.7 copy-done.1
  12.0 0.7 copy-done.2
  12.6 5.5 %shard_map.95.refs_4_ = f32[4,3,136,128]{3,2,1,0:T(8,128)S(1)} custom-call(s32[64]{0:T(128)S(1)} %copy-done.1, s32[64]{0:T(128)S(1)} %copy-done.2, f32[3,4096]{1,0:T(4,128)S(1)} %copy-done, f32[1,4096]{1,0:T(1,128)S(1)} %bitcast.57), custom_call_target="tpu_custom_call" | custom-call | flops 20000000 | bytes 4000000 | tf_op jit(solution)/shard_map/pallas_call | solution.py:111
  18.2 5.5 %shard_map.96 = f32[4,3,136,128]{3,2,1,0:T(8,128)S(1)} custom-call(s32[64]{0:T(128)S(1)} %collective-permute-done.refs_0_, s32[64]{0:T(128)S(1)} %collective-permute-done.1.refs_1_, f32[3,4096]{1,0:T(4,128)S(1)} %collective-permute-done.2.refs_2_, f32[1,4096]{1,0:T(1,128)S(1)} %collective-permute-done.3.refs_3_, f32[4,3,136,128]{3,2,1,0:T(8,128)S(1)} %shard_map.95.refs_4_), custom_call_target="tpu_custom_call" | custom-call | flops 20000000 | bytes 4000000 | tf_op jit(solution)/shard_map/pallas_call | solution.py:111
  23.6 2.9 %convolution_bitcast_fusion = f32[2,1,3,136,512]{4,3,0,2,1:T(8,128)} fusion(f32[4,128,2,512,1]{3,1,0,2,4:T(8,128)S(1)} %copy-done.4, f32[4,3,136,128]{3,2,1,0:T(8,128)S(1)} %shard_map.96), kind=kOutput, calls=%fused_computation.8 | convolution fusion | flops 1283457024 | bytes 4603904 | tf_op jit(solution)/shard_map/tzrl,tlck->czrk/dot_general | solution.py:153
  26.5 4.0 %copy.32 = f32[2,1,3,136,512]{3,0,2,1,4:T(2,128)S(1)} copy(f32[2,1,3,136,512]{4,3,0,2,1:T(8,128)} %convolution_bitcast_fusion) | data formatting | bytes 3342336 | tf_op jit(solution)/shard_map/broadcast_in_dim | solution.py:154
  30.5 39.5 %all_to_all.36 = f32[2,1,3,136,512]{3,0,2,1,4:T(2,128)S(1)} all-to-all(f32[2,1,3,136,512]{3,0,2,1,4:T(2,128)S(1)} %copy.32), channel_id=1, replica_groups=mesh['brick'=8,'pencil'=4] {'pencil'}, dimensions={4} | all-to-all | bytes 3342336 | tf_op jit(solution)/shard_map/all_to_all | solution.py:154
  70.0 0.3 copy.33
  70.3 0.1 slice.36
  70.4 0.5 slice.34
  70.9 0.3 slice_add_fusion
  71.2 1.9 %copy-done.3 = f32[2,2,4,128,512,1]{4,3,2,1,0,5:T(8,128)S(1)} copy-done((f32[2,2,4,128,512,1]{4,3,2,1,0,5:T(8,128)S(1)}, f32[2,2,4,128,512,1]{4,3,2,1,0,5:T(8,128)}, u32[]{:S(2)}) %copy-start.3) | copy-done | bytes 4194328
  73.1 3.1 %fusion.9 = f32[2,3,512,128]{2,3,0,1:T(8,128)S(1)} fusion(f32[2,2,4,128,512,1]{4,3,2,1,0,5:T(8,128)S(1)} %copy-done.3, f32[2,4,3,8,128]{3,4,1,0,2:T(8,128)S(1)} %slice_add_fusion, f32[2,4,3,120,128]{3,4,1,0,2:T(8,128)S(1)} %slice.34), kind=kOutput, calls=%fused_computation.10 | convolution fusion | flops 2416312320 | bytes 7340032 | tf_op jit(solution)/shard_map/dcprk,cpzrx->dzkx/dot_general | solution.py:162
  76.2 2.1 %copy.34 = f32[2,3,512,128]{3,0,1,2:T(2,128)} copy(f32[2,3,512,128]{2,3,0,1:T(8,128)S(1)} %fusion.9) | data formatting | bytes 3145728 | tf_op jit(solution)/shard_map/dcprk,cpzrx->dzkx/transpose | solution.py:162
  78.2 3.8 %all-to-all-start.1 = ((f32[2,3,512,128]{3,0,1,2:T(2,128)}), f32[2,3,512,128]{3,0,1,2:T(2,128)S(1)}, u32[]{:S(2)}, u32[]{:S(2)}) async-start(f32[2,3,512,128]{3,0,1,2:T(2,128)} %copy.34), calls=%async_computation.1 | async-start | bytes 3145728 | tf_op jit(solution)/shard_map/all_to_all | solution.py:163
  82.2 0.1 multiply_divide_fusion
  82.2 0.1 broadcast_add_fusion
  82.3 0.1 broadcast_multiply_fusion
  82.4 36.3 %all-to-all-done.1 = f32[2,3,512,128]{3,0,1,2:T(2,128)S(1)} async-done(((f32[2,3,512,128]{3,0,1,2:T(2,128)}), f32[2,3,512,128]{3,0,1,2:T(2,128)S(1)}, u32[]{:S(2)}, u32[]{:S(2)}) %all-to-all-start.1) | async-done | bytes 1572896 | tf_op jit(solution)/shard_map/all_to_all | solution.py:163
  118.7 0.1 copy.35
  118.8 0.2 copy.36
  119.0 0.6 copy-done.5
  119.6 1.7 %fusion.6 = f32[2,24,64,128]{3,1,2,0:T(8,128)S(1)} fusion(f32[2,2,24,24,1]{2,3,1,4,0:T(8,128)S(1)} %copy-done.5, f32[2,24,64,128]{3,2,1,0:T(8,128)S(1)} %bitcast.62), kind=kOutput, calls=%fused_computation.9 | convolution fusion | flops 113246208 | bytes 3154944 | tf_op jit(solution)/shard_map/dczk,czyx->dkyx/dot_general | solution.py:167
  121.3 1.1 fusion.14
  122.4 1.4 copy.38
  123.8 37.3 %psum.7 = f32[]{:T(128)} all-reduce(f32[]{:T(128)} %fusion.14), channel_id=1, replica_groups=mesh['brick'=8,'pencil'=4] {'brick','pencil'}, use_global_device_ids=true, to_apply=%region_1.2 | all-reduce | flops 1 | bytes 8 | tf_op jit(solution)/shard_map/psum | solution.py:177
  (15 shorter events, 0.2 us)
Async XLA Ops:
  0.6 17.5 %collective-permute-start.2 = (f32[3,4096]{1,0:T(4,128)}, f32[3,4096]{1,0:T(4,128)S(1)}, u32[]{:S(2)}, u32[]{:S(2)}) collective-permute-start(f32[3,4096]{1,0:T(4,128)} %refs_2_.1), channel_id=1, source_target_pairs={{4,0},{8,4},{12,8},{16,12},{20,16},{24,20},{28,24},{0,28},{5,1},{9... | collective-permute-start | bytes 147464 | tf_op jit(solution)/shard_map/ppermute | solution.py:29
  8.1 10.1 %collective-permute-start.3 = (f32[1,4096]{1,0:T(1,128)S(1)}, f32[1,4096]{1,0:T(1,128)S(1)}, u32[]{:S(2)}, u32[]{:S(2)}) collective-permute-start(f32[1,4096]{1,0:T(1,128)S(1)} %bitcast.56), channel_id=1, source_target_pairs={{4,0},{8,4},{12,8},{16,12},{20,16},{24,20},{28,24},{0,28},{5,1},{9... | collective-permute-start | bytes 49160 | tf_op jit(solution)/shard_map/ppermute | solution.py:29
  8.6 9.5 %collective-permute-start = (s32[64]{0:T(128)}, s32[64]{0:T(128)S(1)}, u32[]{:S(2)}, u32[]{:S(2)}) collective-permute-start(s32[64]{0:T(128)} %refs_0_.1), channel_id=1, source_target_pairs={{4,0},{8,4},{12,8},{16,12},{20,16},{24,20},{28,24},{0,28},{5,1},{9... | collective-permute-start | bytes 776 | tf_op jit(solution)/shard_map/ppermute | solution.py:29
  10.0 8.1 %collective-permute-start.1 = (s32[64]{0:T(128)}, s32[64]{0:T(128)S(1)}, u32[]{:S(2)}, u32[]{:S(2)}) collective-permute-start(s32[64]{0:T(128)} %refs_1_.1), channel_id=1, source_target_pairs={{4,0},{8,4},{12,8},{16,12},{20,16},{24,20},{28,24},{0,28},{5,1},{9... | collective-permute-start | bytes 776 | tf_op jit(solution)/shard_map/ppermute | solution.py:29
  10.5 0.8 copy-start
  11.3 0.7 copy-start.1
  12.0 0.7 copy-start.2
  12.6 11.0 %copy-start.4 = (f32[4,128,2,512,1]{3,1,0,2,4:T(8,128)S(1)}, f32[4,128,2,512,1]{3,1,0,2,4:T(8,128)}, u32[]{:S(2)}) copy-start(f32[4,128,2,512,1]{3,1,0,2,4:T(8,128)} %constant.74) | copy-start | bytes 6291460
  70.9 2.2 %copy-start.3 = (f32[2,2,4,128,512,1]{4,3,2,1,0,5:T(8,128)S(1)}, f32[2,2,4,128,512,1]{4,3,2,1,0,5:T(8,128)}, u32[]{:S(2)}) copy-start(f32[2,2,4,128,512,1]{4,3,2,1,0,5:T(8,128)} %constant.75) | copy-start | bytes 12582916
  78.2 40.5 %all-to-all-start.1 = ((f32[2,3,512,128]{3,0,1,2:T(2,128)}), f32[2,3,512,128]{3,0,1,2:T(2,128)S(1)}, u32[]{:S(2)}, u32[]{:S(2)}) async-start(f32[2,3,512,128]{3,0,1,2:T(2,128)} %copy.34), calls=%async_computation.1 | async-start | bytes 3145728 | tf_op jit(solution)/shard_map/all_to_all | solution.py:163
  118.8 0.8 copy-start.5

commit v2 on v1

--- a/solution.py
+++ b/solution.py
@@ -178,6 +178,230 @@
     return total.reshape(1), transformed
 
 
+def wave_terms(length):
+    wave = np.arange(length)
+    fraction = np.where(2 * wave >= length, wave - length, wave) / length
+    fix = 9.0 / (2.0 + np.cos(wave * (FULL_TURN / length))) ** 2
+    weight = fix * np.exp(-(math.pi**2) / EWALD_SPLIT**2 * fraction**2)
+    return (fraction**2).astype(np.float32), weight.astype(np.float32)
+
+
+def by_factor(value, angle):
+    cosine, sine = math.cos(angle), math.sin(angle)
+    real, imag = value
+    if abs(sine) < 1e-12 and cosine > 0.0:
+        return value
+    if abs(cosine) < 1e-12 and sine > 0.0:
+        return imag, -real
+    return real * cosine + imag * sine, imag * cosine - real * sine
+
+
+def radix_two(values):
+    count = len(values)
+    if count == 1:
+        return values
+    even, odd = radix_two(values[0::2]), radix_two(values[1::2])
+    odd = [by_factor(value, FULL_TURN * k / count) for k, value in enumerate(odd)]
+    first = [(a[0] + b[0], a[1] + b[1]) for a, b in zip(even, odd)]
+    return first + [(a[0] - b[0], a[1] - b[1]) for a, b in zip(even, odd)]
+
+
+def leading_transform(planes):
+    bricks = len(planes[0])
+    length = ZDEV * bricks
+    parts = [radix_two(plane) for plane in planes]
+    result = [None] * length
+    for k in range(bricks):
+        base = parts[0][k]
+        one = by_factor(parts[1][k], FULL_TURN * k / length)
+        two = by_factor(parts[2][k], FULL_TURN * 2 * k / length)
+        total = (one[0] + two[0], one[1] + two[1])
+        apart = ((one[0] - two[0]) * (0.5 * math.sqrt(3.0)), (one[1] - two[1]) * (0.5 * math.sqrt(3.0)))
+        middle = (base[0] - 0.5 * total[0], base[1] - 0.5 * total[1])
+        result[k] = (base[0] + total[0], base[1] + total[1])
+        result[k + bricks] = (middle[0] + apart[1], middle[1] - apart[0])
+        result[k + 2 * bricks] = (middle[0] - apart[1], middle[1] + apart[0])
+    return result
+
+
+def fused_kernel(
+    pencils, bricks,
+    grid_ref, xhigh_ref, xlow_ref, yhigh_ref, ylow_ref, yterm_ref, xterm_ref,
+    energy_ref, spectrum_ref,
+    xs, xr, ys, zr, ep, eb,
+    xsend, xrecv, zsend, zrecv, epsend, eprecv, ebsend, ebrecv,
+):
+    mine = {"pencil": lax.axis_index("pencil"), "brick": lax.axis_index("brick")}
+    sizes = {"pencil": pencils, "brick": bricks}
+    part = NY // bricks
+    rows = NY // pencils
+    started = []
+
+    def peer(axis, step):
+        return lax.rem(mine[axis] + step, sizes[axis])
+
+    def send(axis, step, source, target, send_sem, recv_sem):
+        copy = pltpu.make_async_remote_copy(
+            src_ref=source, dst_ref=target, send_sem=send_sem, recv_sem=recv_sem,
+            device_id={axis: peer(axis, step)}, device_id_type=pl.DeviceIdType.MESH,
+        )
+        copy.start()
+        started.append(copy)
+
+    def arrived(axis, step, target, recv_sem, send_sem):
+        pltpu.make_async_remote_copy(
+            src_ref=target, dst_ref=target, send_sem=send_sem, recv_sem=recv_sem,
+            device_id={axis: peer(axis, step)}, device_id_type=pl.DeviceIdType.MESH,
+        ).wait_recv()
+
+    barrier = pltpu.get_barrier_semaphore()
+    for axis in sizes:
+        for step in range(1, sizes[axis]):
+            pl.semaphore_signal(
+                barrier, inc=1, device_id={axis: peer(axis, step)},
+                device_id_type=pl.DeviceIdType.MESH,
+            )
+
+    me, slab = mine["pencil"], mine["brick"]
+    for plane in range(ZDEV):
+        lines = jnp.concatenate([grid_ref[t, plane] for t in range(NX // LANES)], axis=1)
+        after_x = dot3(split(lines), (xhigh_ref[...], xlow_ref[...]), ((1,), (0,)))
+        width = after_x.shape[1] // pencils
+        for target in range(pencils):
+            xs[plane, target] = after_x[:, target * width : (target + 1) * width]
+        if plane == 0:
+            pl.semaphore_wait(barrier, pencils + bricks - 2)
+        for step in range(1, pencils):
+            send(
+                "pencil", step, xs.at[plane, peer("pencil", step)], xr.at[plane, me],
+                xsend.at[plane, step], xrecv.at[plane, me],
+            )
+        xr[plane, me] = xs[plane, me]
+
+    for plane in range(ZDEV):
+        for step in range(1, pencils):
+            other = peer("pencil", step)
+            arrived("pencil", step, xr.at[plane, other], xrecv.at[plane, other], xsend.at[plane, step])
+        pieces = []
+        for source in range(pencils):
+            pieces.append(xr[plane, source, RIM:rows])
+            rim = xr[plane, (source + 1) % pencils, 0:RIM]
+            pieces.append(xr[plane, source, rows : rows + RIM] + rim)
+        columns = split(jnp.concatenate(pieces, axis=0))
+        both = dot3((yhigh_ref[...], ylow_ref[...]), columns, ((1,), (0,)))
+        real = both[:NY, :LANES] + both[NY:, LANES:]
+        imag = both[:NY, LANES:] - both[NY:, :LANES]
+        for target in range(bricks):
+            ys[plane, target, :, 0:LANES] = real[target * part : (target + 1) * part]
+            ys[plane, target, :, LANES:] = imag[target * part : (target + 1) * part]
+        for step in range(1, bricks):
+            send(
+                "brick", step, ys.at[plane, peer("brick", step)], zr.at[plane, slab],
+                zsend.at[plane, step], zrecv.at[plane, slab],
+            )
+        zr[plane, slab] = ys[plane, slab]
+
+    for plane in range(ZDEV):
+        for step in range(1, bricks):
+            other = peer("brick", step)
+            arrived("brick", step, zr.at[plane, other], zrecv.at[plane, other], zsend.at[plane, step])
+
+    length = ZDEV * bricks
+    depth_square, depth_weight = wave_terms(length)
+    lanes = pl.ds(pl.multiple_of(me * LANES, LANES), LANES)
+
+    def chunk(step, total):
+        here = pl.ds(pl.multiple_of(step * 8, 8), 8)
+        planes = [
+            [(zr[i, b, here, 0:LANES], zr[i, b, here, LANES : 2 * LANES]) for b in range(bricks)]
+            for i in range(ZDEV)
+        ]
+        result = leading_transform(planes)
+        across = pl.ds(pl.multiple_of(slab * part + step * 8, 8), 8)
+        square = yterm_ref[0, across, :] + xterm_ref[0, :, lanes]
+        weight = yterm_ref[1, across, :] * xterm_ref[1, :, lanes]
+        powers = {}
+        for k, (real, imag) in enumerate(result):
+            spectrum_ref[0, k, here, :] = real
+            spectrum_ref[1, k, here, :] = imag
+            fold = min(k, length - k)
+            powers[fold] = powers.get(fold, 0.0) + (real * real + imag * imag)
+        inner = jnp.zeros_like(total)
+        for k, power in powers.items():
+            q = square + float(depth_square[k])
+            term = float(depth_weight[k]) * power / jnp.where(q == 0.0, 1.0, q)
+            inner = inner + (jnp.where(q == 0.0, 0.0, term) if k == 0 else term)
+        return total + inner * weight
+
+    share = lax.fori_loop(0, part // 8, chunk, jnp.zeros((8, LANES), jnp.float32))
+    share = share * (1.0 / (math.pi * (length * NY * NX)))
+    for axis, held, sends, recvs in (
+        ("pencil", ep, epsend, eprecv), ("brick", eb, ebsend, ebrecv),
+    ):
+        own = mine[axis]
+        held[own] = share
+        for step in range(1, sizes[axis]):
+            send(axis, step, held.at[own], held.at[own], sends.at[step], recvs.at[own])
+        for step in range(1, sizes[axis]):
+            other = peer(axis, step)
+            arrived(axis, step, held.at[other], recvs.at[other], sends.at[step])
+        share = held[0]
+        for source in range(1, sizes[axis]):
+            share = share + held[source]
+    energy_ref[...] = share
+    for copy in started:
+        copy.wait_send()
+
+
+def transform_fused(grid, rows):
+    pencils, bricks = lax.axis_size("pencil"), lax.axis_size("brick")
+    part = NY // bricks
+    columns = NX // pencils
+    cosine, sine = tables(NX)
+    turn_x = np.stack(
+        [cosine.reshape(NX, pencils, columns), -sine.reshape(NX, pencils, columns)], axis=2
+    ).reshape(NX, 2 * NX)
+    cosine, sine = tables(NY)
+    turn_y = np.concatenate([cosine, sine], axis=0)
+
+    def halves(table):
+        high = table.astype(jnp.bfloat16)
+        return high, (table - high.astype(np.float32)).astype(jnp.bfloat16)
+
+    y_terms = np.broadcast_to(np.stack(wave_terms(NY))[:, :, None], (2, NY, LANES))
+    x_terms = np.broadcast_to(np.stack(wave_terms(NX))[:, None, :], (2, 8, NX))
+    f32 = jnp.float32
+    whole = pl.BlockSpec(memory_space=pltpu.VMEM)
+    dma = pltpu.SemaphoreType.DMA
+    energy, spectrum = pl.pallas_call(
+        functools.partial(fused_kernel, pencils, bricks),
+        out_shape=(
+            jax.ShapeDtypeStruct((8, LANES), f32),
+            jax.ShapeDtypeStruct((2, ZDEV * bricks, part, columns), f32),
+        ),
+        in_specs=[whole] * 7,
+        out_specs=(whole, whole),
+        scratch_shapes=[
+            pltpu.VMEM((ZDEV, pencils, rows + RIM, 2 * LANES), f32),
+            pltpu.VMEM((ZDEV, pencils, rows + RIM, 2 * LANES), f32),
+            pltpu.VMEM((ZDEV, bricks, part, 2 * LANES), f32),
+            pltpu.VMEM((ZDEV, bricks, part, 2 * LANES), f32),
+            pltpu.VMEM((pencils, 8, LANES), f32),
+            pltpu.VMEM((bricks, 8, LANES), f32),
+            dma((ZDEV, pencils)), dma((ZDEV, pencils)),
+            dma((ZDEV, bricks)), dma((ZDEV, bricks)),
+            dma((pencils,)), dma((pencils,)), dma((bricks,)), dma((bricks,)),
+        ],
+        compiler_params=pltpu.CompilerParams(
+            collective_id=0, has_side_effects=True, vmem_limit_bytes=40 * 1024 * 1024
+        ),
+        cost_estimate=pl.CostEstimate(
+            flops=6_000_000_000, bytes_accessed=8_000_000, transcendentals=0
+        ),
+    )(grid, *halves(turn_x), *halves(turn_y), y_terms.astype(np.float32), x_terms.astype(np.float32))
+    return jnp.sum(energy).reshape(1), spectrum
+
+
 def shards(positions, charges, anchor_row, anchor_column, counts):
     slot_count = anchor_row.shape[0]
     atoms = charges.shape[0]
@@ -190,7 +414,12 @@
     ]
     grid = spread(3, rows, anchor_row, anchor_column, positions, charge)
     grid = spread(0, rows, *other, grid)
-    total, spectrum = transform_by_steps(grid, rows)
+    bricks = lax.axis_size("brick")
+    tiled = NX // lax.axis_size("pencil") == LANES and NY // bricks % 8 == 0
+    if tiled and bricks & (bricks - 1) == 0:
+        total, spectrum = transform_fused(grid, rows)
+    else:
+        total, spectrum = transform_by_steps(grid, rows)
     slot_total = slot_count * lax.axis_size("brick") * lax.axis_size("pencil")
     return (total * (0.5 / slot_total), spectrum)
 

time: 164 us -> 83.2 us (0.51)
  blocking collectives: 76.8 us -> 0 us
  Pallas kernels: 10.9 us -> 64.1 us
  waiting for transfers between devices: 36.3 us -> 0.01 us
  local copies, waits for them, and re-layouts: 13.4 us -> 5.76 us
  matrix products: 7.62 us -> 0 us
  starting transfers between devices: 12.3 us -> 8.48 us
    pallas_call x0 -> x1, Pallas kernels: none -> 53.2 us  [transform_fused(): pl.pallas_call(functools.partial(fused_kernel, pencils, bricks), out_shap...]
    all_to_all x1 -> x0, blocking collectives: 39.5 us -> none  [transform_by_steps(): lax.all_to_all(after_x[:, None], 'pencil', split_axis=4, concat_axis=1, t...]
    psum x1 -> x0, blocking collectives: 37.3 us -> none  [transform_by_steps(): total = lax.psum(jnp.sum(kernel * power), ('brick', 'pencil'))]
    all_to_all x1 -> x0, waiting for transfers between devices: 36.3 us -> none  [transform_by_steps(): lax.all_to_all(after_y, 'brick', split_axis=2, concat_axis=1, tiled=True)]
    dot_general x3 -> x0, matrix products: 7.62 us -> none  [the longest x1 3.06 us: transform_by_steps(): after_y = jnp.einsum('dcprk,cpzrx->dzkx', turn, body, precision=HIGH)]
    broadcast_in_dim x1 -> x0, local copies, waits for them, and re-layouts: 3.99 us -> none  [transform_by_steps(): after_x[:, None]]
    all_to_all x1 -> x0, starting transfers between devices: 3.8 us -> none  [transform_by_steps(): lax.all_to_all(after_y, 'brick', split_axis=2, concat_axis=1, tiled=True)]
    transpose x1 -> x0, local copies, waits for them, and re-layouts: 2.08 us -> none  [transform_by_steps(): after_y = jnp.einsum('dcprk,cpzrx->dzkx', turn, body, precision=HIGH)]
  transfers between devices with their start and end apart: 5 -> 4, of which waited for: 1 -> 0; matrix products, arithmetic and copies ran while one was open for 1% -> 1% of each run, Pallas kernels for 3% -> 7%
where the time goes in v2:
time: 83.2 us; the launch traced here: 82.9 us
  Pallas kernels  64.1 us (77%)
  starting transfers between devices  8.48 us (10%)
  local copies, waits for them, and re-layouts  5.76 us (7%)
  between operations  3.18 us (4%)
  other arithmetic  1.32 us (2%)
    pallas_call x1, Pallas kernels, transform_fused(): pl.pallas_call(functools.partial(fused_kernel, pencils, bricks), out_shap...  53.2 us
    pallas_call x2, Pallas kernels, spread(): pl.pallas_call(functools.partial(spread_kernel, first_plane, charge.shape...  10.9 us
    ppermute x4, starting transfers between devices, from_behind(): return lax.ppermute(block, axis, route)  8.48 us
    unnamed x19, local copies, waits for them, and re-layouts  5.76 us
  transfers between devices with their start and end apart: 4, of which 0 were waited for; matrix products, arithmetic and copies ran while one was open for 1% of the time, Pallas kernels for 7%

profile of v2, /device:TPU:0, one launch (start us, length us, event | category | flops | bytes accessed | tf_op | source)
XLA Modules:
  0.0 82.9 jit_solution(15887764197112332168)
XLA Ops:
  0.6 0.0 copy-start.8
  0.6 6.1 %collective-permute-start.2 = (f32[3,4096]{1,0:T(4,128)}, f32[3,4096]{1,0:T(4,128)S(1)}, u32[]{:S(2)}, u32[]{:S(2)}) collective-permute-start(f32[3,4096]{1,0:T(4,128)} %refs_2_.1), channel_id=1, source_target_pairs={{4,0},{8,4},{12,8},{16,12},{20,16},{24,20},{28,24},{0,28},{5,1},{9... | collective-permute-start | bytes 147464 | tf_op jit(solution)/shard_map/ppermute | solution.py:29
  7.4 0.7 fusion
  8.1 0.5 collective-permute-start.3
  8.6 1.4 %collective-permute-start = (s32[64]{0:T(128)}, s32[64]{0:T(128)S(1)}, u32[]{:S(2)}, u32[]{:S(2)}) collective-permute-start(s32[64]{0:T(128)} %refs_0_.1), channel_id=1, source_target_pairs={{4,0},{8,4},{12,8},{16,12},{20,16},{24,20},{28,24},{0,28},{5,1},{9... | collective-permute-start | bytes 776 | tf_op jit(solution)/shard_map/ppermute | solution.py:29
  10.0 0.5 collective-permute-start.1
  10.5 0.0 copy-start
  10.5 0.8 %copy-done = f32[3,4096]{1,0:T(4,128)S(1)} copy-done((f32[3,4096]{1,0:T(4,128)S(1)}, f32[3,4096]{1,0:T(4,128)}, u32[]{:S(2)}) %copy-start) | copy-done | bytes 49176
  11.3 0.0 copy-start.1
  11.3 0.7 copy-done.1
  12.0 0.0 copy-start.2
  12.0 0.7 copy-done.2
  12.6 0.0 copy-start.3
  12.6 0.0 copy-start.4
  12.7 0.0 copy-start.7
  12.7 5.5 %shard_map.122.refs_4_ = f32[4,3,136,128]{3,2,1,0:T(8,128)S(1)} custom-call(s32[64]{0:T(128)S(1)} %copy-done.1, s32[64]{0:T(128)S(1)} %copy-done.2, f32[3,4096]{1,0:T(4,128)S(1)} %copy-done, f32[1,4096]{1,0:T(1,128)S(1)} %bitcast.4), custom_call_target="tpu_custom_call" | custom-call | flops 20000000 | bytes 4000000 | tf_op jit(solution)/shard_map/pallas_call | solution.py:111
  18.1 0.0 collective-permute-done.refs_0_
  18.1 0.0 collective-permute-done.1.refs_1_
  18.1 0.0 collective-permute-done.3.refs_3_
  18.2 0.0 collective-permute-done.2.refs_2_
  18.2 5.5 %shard_map.123.grid_ref = f32[4,3,136,128]{3,2,1,0:T(8,128)S(1)} custom-call(s32[64]{0:T(128)S(1)} %collective-permute-done.refs_0_, s32[64]{0:T(128)S(1)} %collective-permute-done.1.refs_1_, f32[3,4096]{1,0:T(4,128)S(1)} %collective-permute-done.2.refs_2_, f32[1,4096]{1,0:T(1,128)S(1)} %collective-permute-done.3.refs_3_, ...), custom_call_target="tpu_custom_call" | custom-call | flops 20000000 | bytes 4000000 | tf_op jit(solution)/shard_map/pallas_call | solution.py:111
  23.7 0.0 copy-done.8
  23.7 0.0 copy-done.3
  23.7 0.0 copy-done.4
  23.7 0.0 copy-done.7
  23.7 0.0 copy-start.5
  23.7 1.2 %copy-done.5 = bf16[512,1024]{1,0:T(8,128)(2,1)S(1)} copy-done((bf16[512,1024]{1,0:T(8,128)(2,1)S(1)}, bf16[512,1024]{1,0:T(8,128)(2,1)}, u32[]{:S(2)}) %copy-start.5) | copy-done | bytes 1048600
  24.9 0.0 copy-start.6
  24.9 1.2 %copy-done.6 = bf16[512,1024]{1,0:T(8,128)(2,1)S(1)} copy-done((bf16[512,1024]{1,0:T(8,128)(2,1)S(1)}, bf16[512,1024]{1,0:T(8,128)(2,1)}, u32[]{:S(2)}) %copy-start.6) | copy-done | bytes 1048600
  26.1 53.2 %shard_map.124 = (f32[8,128]{1,0:T(8,128)S(1)}, f32[2,24,64,128]{3,2,1,0:T(8,128)S(1)}) custom-call(f32[4,3,136,128]{3,2,1,0:T(8,128)S(1)} %shard_map.123.grid_ref, bf16[512,1024]{1,0:T(8,128)(2,1)S(1)} %copy-done.6, bf16[512,1024]{1,0:T(8,128)(2,1)S(1)} %copy-done.5, bf16[1024,512]{1,0:T(8,128)(2,1)S(1)} %copy-done.4, bf16[1024,512]{1,0:T(8,128)(2,1)S(1)} %copy-done.3, ...), custom_call_target="tpu_custom_call" | custom-call | flops 6000000000 | bytes 8000000 | tf_op jit(solution)/shard_map/pallas_call | solution.py:376
  79.4 0.6 reduce_sum.9
  80.6 1.1 %copy.15 = f32[2,24,64,128]{3,2,1,0:T(8,128)} copy(f32[2,24,64,128]{3,2,1,0:T(8,128)S(1)} %get-tuple-element.9) | data formatting | bytes 3145728
Async XLA Ops:
  0.6 23.0 %copy-start.8 = (f32[2,8,512]{2,1,0:T(8,128)S(1)}, f32[2,8,512]{2,1,0:T(8,128)}, u32[]{:S(2)}) copy-start(f32[2,8,512]{2,1,0:T(8,128)} %constant.26.clone.xterm_ref) | copy-start | bytes 98308
  0.6 17.5 %collective-permute-start.2 = (f32[3,4096]{1,0:T(4,128)}, f32[3,4096]{1,0:T(4,128)S(1)}, u32[]{:S(2)}, u32[]{:S(2)}) collective-permute-start(f32[3,4096]{1,0:T(4,128)} %refs_2_.1), channel_id=1, source_target_pairs={{4,0},{8,4},{12,8},{16,12},{20,16},{24,20},{28,24},{0,28},{5,1},{9... | collective-permute-start | bytes 147464 | tf_op jit(solution)/shard_map/ppermute | solution.py:29
  8.1 10.1 %collective-permute-start.3 = (f32[1,4096]{1,0:T(1,128)S(1)}, f32[1,4096]{1,0:T(1,128)S(1)}, u32[]{:S(2)}, u32[]{:S(2)}) collective-permute-start(f32[1,4096]{1,0:T(1,128)S(1)} %bitcast.3), channel_id=1, source_target_pairs={{4,0},{8,4},{12,8},{16,12},{20,16},{24,20},{28,24},{0,28},{5,1},{9... | collective-permute-start | bytes 49160 | tf_op jit(solution)/shard_map/ppermute | solution.py:29
  8.6 9.5 %collective-permute-start = (s32[64]{0:T(128)}, s32[64]{0:T(128)S(1)}, u32[]{:S(2)}, u32[]{:S(2)}) collective-permute-start(s32[64]{0:T(128)} %refs_0_.1), channel_id=1, source_target_pairs={{4,0},{8,4},{12,8},{16,12},{20,16},{24,20},{28,24},{0,28},{5,1},{9... | collective-permute-start | bytes 776 | tf_op jit(solution)/shard_map/ppermute | solution.py:29
  10.0 8.1 %collective-permute-start.1 = (s32[64]{0:T(128)}, s32[64]{0:T(128)S(1)}, u32[]{:S(2)}, u32[]{:S(2)}) collective-permute-start(s32[64]{0:T(128)} %refs_1_.1), channel_id=1, source_target_pairs={{4,0},{8,4},{12,8},{16,12},{20,16},{24,20},{28,24},{0,28},{5,1},{9... | collective-permute-start | bytes 776 | tf_op jit(solution)/shard_map/ppermute | solution.py:29
  10.5 0.8 %copy-start = (f32[3,4096]{1,0:T(4,128)S(1)}, f32[3,4096]{1,0:T(4,128)}, u32[]{:S(2)}) copy-start(f32[3,4096]{1,0:T(4,128)} %refs_2_.1) | copy-start | bytes 147460
  11.3 0.7 copy-start.1
  12.0 0.7 copy-start.2
  12.6 11.0 %copy-start.3 = (bf16[1024,512]{1,0:T(8,128)(2,1)S(1)}, bf16[1024,512]{1,0:T(8,128)(2,1)}, u32[]{:S(2)}) copy-start(bf16[1024,512]{1,0:T(8,128)(2,1)} %constant.24.clone.ylow_ref) | copy-start | bytes 3145732
  12.6 11.0 %copy-start.4 = (bf16[1024,512]{1,0:T(8,128)(2,1)S(1)}, bf16[1024,512]{1,0:T(8,128)(2,1)}, u32[]{:S(2)}) copy-start(bf16[1024,512]{1,0:T(8,128)(2,1)} %constant.23.clone.yhigh_ref) | copy-start | bytes 3145732
  12.7 11.0 %copy-start.7 = (f32[2,512,128]{2,1,0:T(8,128)S(1)}, f32[2,512,128]{2,1,0:T(8,128)}, u32[]{:S(2)}) copy-start(f32[2,512,128]{2,1,0:T(8,128)} %constant.25.clone.yterm_ref) | copy-start | bytes 1572868
  23.7 1.2 %copy-start.5 = (bf16[512,1024]{1,0:T(8,128)(2,1)S(1)}, bf16[512,1024]{1,0:T(8,128)(2,1)}, u32[]{:S(2)}) copy-start(bf16[512,1024]{1,0:T(8,128)(2,1)} %constant.22.clone.xlow_ref) | copy-start | bytes 3145732
  24.9 1.2 %copy-start.6 = (bf16[512,1024]{1,0:T(8,128)(2,1)S(1)}, bf16[512,1024]{1,0:T(8,128)(2,1)}, u32[]{:S(2)}) copy-start(bf16[512,1024]{1,0:T(8,128)(2,1)} %constant.21.clone.xhigh_ref) | copy-start | bytes 3145732

commit v3 on v2

--- a/solution.py
+++ b/solution.py
@@ -50,8 +50,8 @@
 
 
 def spread_kernel(first_plane, block_atoms, *refs):
-    row_ref, column_ref, coords_ref, charge_ref, *before, grid_ref = refs
-    slots = row_ref.shape[0]
+    anchor_ref, coords_ref, *before, grid_ref = refs
+    slots = anchor_ref.shape[0] // 2
     if before:
         grid_ref[...] = before[0][...]
     else:
@@ -66,7 +66,7 @@
 
     def turn(step, carry):
         here = pl.ds(pl.multiple_of(step * width, width), width)
-        depth = spline(coords_ref[0:1, here] - planes) * charge_ref[0:1, here]
+        depth = spline(coords_ref[0:1, here] - planes) * coords_ref[3:4, here]
         lines = spline(coords_ref[1:2, here] - steps)
         cells = split(spline(coords_ref[2:3, here] - steps))
         cells = [jnp.concatenate([part, blank], axis=0) for part in cells]
@@ -79,8 +79,8 @@
         values = dot3(sheets, cells, ((1,), (1,)))
         for member in range(GROUP):
             block = step * GROUP + member
-            column = column_ref[block]
-            row = row_ref[block] + (RIM - 3)
+            column = anchor_ref[slots + block]
+            row = anchor_ref[block] + (RIM - 3)
             shift = column & (LANES - 1)
             tile = column // LANES
             over = (tile + 1) & (tiles - 1)
@@ -100,24 +100,24 @@
                     grid_ref[where, plane, pl.ds(row, PY), :] = sums[index * ZDEV + plane]
         return carry
 
-    lax.fori_loop(0, slots // GROUP, turn, 0)
-
-
-def spread(first_plane, rows, anchor_row, anchor_column, coords, charge, *before):
-    slots = anchor_row.shape[0]
+    lax.fori_loop(0, slots // GROUP, turn, 0, unroll=4)
+
+
+def spread(first_plane, rows, anchors, coords, *before):
+    slots = anchors.shape[0] // 2
     shape = (NX // LANES, ZDEV, rows + RIM, LANES)
     scalar = pl.BlockSpec(memory_space=pltpu.SMEM)
     whole = pl.BlockSpec(memory_space=pltpu.VMEM)
     return pl.pallas_call(
-        functools.partial(spread_kernel, first_plane, charge.shape[1] // slots),
+        functools.partial(spread_kernel, first_plane, coords.shape[1] // slots),
         out_shape=jax.ShapeDtypeStruct(shape, jnp.float32),
-        in_specs=[scalar, scalar] + [whole] * (2 + len(before)),
+        in_specs=[scalar] + [whole] * (1 + len(before)),
         out_specs=whole,
-        compiler_params=pltpu.CompilerParams(vmem_limit_bytes=24 * 1024 * 1024),
+        compiler_params=pltpu.CompilerParams(vmem_limit_bytes=10 * 1024 * 1024),
         cost_estimate=pl.CostEstimate(
             flops=20_000_000, bytes_accessed=4_000_000, transcendentals=0
         ),
-    )(anchor_row, anchor_column, coords, charge, *before)
+    )(anchors, coords, *before)
 
 
 def terms_of(wave_index, length):
@@ -206,10 +206,9 @@
     return first + [(a[0] - b[0], a[1] - b[1]) for a, b in zip(even, odd)]
 
 
-def leading_transform(planes):
-    bricks = len(planes[0])
+def leading_transform(parts):
+    bricks = len(parts[0])
     length = ZDEV * bricks
-    parts = [radix_two(plane) for plane in planes]
     result = [None] * length
     for k in range(bricks):
         base = parts[0][k]
@@ -226,9 +225,9 @@
 
 def fused_kernel(
     pencils, bricks,
-    grid_ref, xhigh_ref, xlow_ref, yhigh_ref, ylow_ref, yterm_ref, xterm_ref,
+    grid_ref, xhigh_ref, xlow_ref, yhigh_any, ylow_any, yterm_any, xterm_ref,
     energy_ref, spectrum_ref,
-    xs, xr, ys, zr, ep, eb,
+    yhigh_ref, ylow_ref, yterm_ref, fetched, xs, xr, ys, zr, ep, eb,
     xsend, xrecv, zsend, zrecv, epsend, eprecv, ebsend, ebrecv,
 ):
     mine = {"pencil": lax.axis_index("pencil"), "brick": lax.axis_index("brick")}
@@ -238,7 +237,11 @@
     started = []
 
     def peer(axis, step):
-        return lax.rem(mine[axis] + step, sizes[axis])
+        half = sizes[axis] // 2
+        side, place = mine[axis] // half, mine[axis] % half
+        if step <= half:
+            return (1 - side) * half + lax.rem(place + step - 1, half)
+        return side * half + lax.rem(place + step - half, half)
 
     def send(axis, step, source, target, send_sem, recv_sem):
         copy = pltpu.make_async_remote_copy(
@@ -254,6 +257,14 @@
             device_id={axis: peer(axis, step)}, device_id_type=pl.DeviceIdType.MESH,
         ).wait_recv()
 
+    fetches = [
+        pltpu.make_async_copy(source, target, fetched.at[i])
+        for i, (source, target) in enumerate(
+            [(yhigh_any, yhigh_ref), (ylow_any, ylow_ref), (yterm_any, yterm_ref)]
+        )
+    ]
+    for fetch in fetches:
+        fetch.start()
     barrier = pltpu.get_barrier_semaphore()
     for axis in sizes:
         for step in range(1, sizes[axis]):
@@ -263,6 +274,14 @@
             )
 
     me, slab = mine["pencil"], mine["brick"]
+
+    def send_lines(plane):
+        for step in range(1, pencils):
+            send(
+                "pencil", step, xs.at[plane, peer("pencil", step)], xr.at[plane, me],
+                xsend.at[plane, step], xrecv.at[plane, me],
+            )
+
     for plane in range(ZDEV):
         lines = jnp.concatenate([grid_ref[t, plane] for t in range(NX // LANES)], axis=1)
         after_x = dot3(split(lines), (xhigh_ref[...], xlow_ref[...]), ((1,), (0,)))
@@ -271,17 +290,18 @@
             xs[plane, target] = after_x[:, target * width : (target + 1) * width]
         if plane == 0:
             pl.semaphore_wait(barrier, pencils + bricks - 2)
-        for step in range(1, pencils):
-            send(
-                "pencil", step, xs.at[plane, peer("pencil", step)], xr.at[plane, me],
-                xsend.at[plane, step], xrecv.at[plane, me],
-            )
+            send_lines(plane)
         xr[plane, me] = xs[plane, me]
 
     for plane in range(ZDEV):
         for step in range(1, pencils):
             other = peer("pencil", step)
             arrived("pencil", step, xr.at[plane, other], xrecv.at[plane, other], xsend.at[plane, step])
+        if plane + 1 < ZDEV:
+            send_lines(plane + 1)
+        if plane == 0:
+            for fetch in fetches:
+                fetch.wait()
         pieces = []
         for source in range(pencils):
             pieces.append(xr[plane, source, RIM:rows])
@@ -301,10 +321,23 @@
             )
         zr[plane, slab] = ys[plane, slab]
 
+    def over_bricks(plane, step, carry):
+        here = pl.ds(pl.multiple_of(step * 8, 8), 8)
+        values = [
+            (zr[plane, b, here, 0:LANES], zr[plane, b, here, LANES : 2 * LANES])
+            for b in range(bricks)
+        ]
+        for k, (real, imag) in enumerate(radix_two(values)):
+            zr[plane, k, here, 0:LANES] = real
+            zr[plane, k, here, LANES : 2 * LANES] = imag
+        return carry
+
     for plane in range(ZDEV):
         for step in range(1, bricks):
             other = peer("brick", step)
             arrived("brick", step, zr.at[plane, other], zrecv.at[plane, other], zsend.at[plane, step])
+        if plane + 1 < ZDEV:
+            lax.fori_loop(0, part // 8, functools.partial(over_bricks, plane), 0)
 
     length = ZDEV * bricks
     depth_square, depth_weight = wave_terms(length)
@@ -316,7 +349,7 @@
             [(zr[i, b, here, 0:LANES], zr[i, b, here, LANES : 2 * LANES]) for b in range(bricks)]
             for i in range(ZDEV)
         ]
-        result = leading_transform(planes)
+        result = leading_transform(planes[:-1] + [radix_two(planes[-1])])
         across = pl.ds(pl.multiple_of(slab * part + step * 8, 8), 8)
         square = yterm_ref[0, across, :] + xterm_ref[0, :, lanes]
         weight = yterm_ref[1, across, :] * xterm_ref[1, :, lanes]
@@ -379,9 +412,13 @@
             jax.ShapeDtypeStruct((8, LANES), f32),
             jax.ShapeDtypeStruct((2, ZDEV * bricks, part, columns), f32),
         ),
-        in_specs=[whole] * 7,
+        in_specs=[whole] * 3 + [pl.BlockSpec(memory_space=pl.ANY)] * 3 + [whole],
         out_specs=(whole, whole),
         scratch_shapes=[
+            pltpu.VMEM((2 * NY, NY), jnp.bfloat16),
+            pltpu.VMEM((2 * NY, NY), jnp.bfloat16),
+            pltpu.VMEM((2, NY, LANES), f32),
+            dma((3,)),
             pltpu.VMEM((ZDEV, pencils, rows + RIM, 2 * LANES), f32),
             pltpu.VMEM((ZDEV, pencils, rows + RIM, 2 * LANES), f32),
             pltpu.VMEM((ZDEV, bricks, part, 2 * LANES), f32),
@@ -393,7 +430,7 @@
             dma((pencils,)), dma((pencils,)), dma((bricks,)), dma((bricks,)),
         ],
         compiler_params=pltpu.CompilerParams(
-            collective_id=0, has_side_effects=True, vmem_limit_bytes=40 * 1024 * 1024
+            collective_id=0, has_side_effects=True, vmem_limit_bytes=24 * 1024 * 1024
         ),
         cost_estimate=pl.CostEstimate(
             flops=6_000_000_000, bytes_accessed=8_000_000, transcendentals=0
@@ -409,11 +446,12 @@
     rows = NY // lax.axis_size("pencil")
     live = jnp.arange(atoms, dtype=jnp.int32) < counts[0] * block_atoms
     charge = (charges * live.astype(jnp.float32)).reshape(1, atoms)
-    other = [
-        from_behind(array, "brick", -1) for array in (anchor_row, anchor_column, positions, charge)
-    ]
-    grid = spread(3, rows, anchor_row, anchor_column, positions, charge)
-    grid = spread(0, rows, *other, grid)
+    coords = jnp.concatenate([positions, charge], axis=0)
+    anchors = jnp.concatenate([anchor_row, anchor_column])
+    grid = spread(3, rows, anchors, coords)
+    grid, anchors, coords = lax.optimization_barrier((grid, anchors, coords))
+    anchors, coords = (from_behind(array, "brick", -1) for array in (anchors, coords))
+    grid = spread(0, rows, anchors, coords, grid)
     bricks = lax.axis_size("brick")
     tiled = NX // lax.axis_size("pencil") == LANES and NY // bricks % 8 == 0
     if tiled and bricks & (bricks - 1) == 0:

time: 83.2 us -> 78.7 us (0.946)
  Pallas kernels: 64.1 us -> 58.9 us
  waiting for transfers between devices: 0.01 us -> 3.04 us
  local copies, waits for them, and re-layouts: 5.76 us -> 3.62 us
  starting transfers between devices: 8.48 us -> 6.56 us
  other arithmetic: 1.32 us -> 2.94 us
    pallas_call x2, Pallas kernels: 10.9 us -> 5.9 us  [spread(): pl.pallas_call(functools.partial(spread_kernel, first_plane, coords.shape...]
    ppermute x4 -> x2, waiting for transfers between devices: 0.01 us -> 3.04 us  [from_behind(): return lax.ppermute(block, axis, route)]
    unnamed x19 -> x13, local copies, waits for them, and re-layouts: 5.76 us -> 3.62 us
    ppermute x4 -> x2, starting transfers between devices: 8.48 us -> 6.56 us  [from_behind(): return lax.ppermute(block, axis, route)]
    concatenate x0 -> x2, other arithmetic: none -> 1.62 us  [the longest x1 0.87 us: shards(): coords = jnp.concatenate([positions, charge], axis=0)]
  transfers between devices with their start and end apart: 4 -> 2, of which waited for: 0 -> 1; matrix products, arithmetic and copies ran while one was open for 1% -> 0% of each run, Pallas kernels for 7% -> 0%
where the time goes in v3:
time: 78.7 us; the launch traced here: 78.3 us
  Pallas kernels  58.9 us (75%)
  starting transfers between devices  6.56 us (8%)
  local copies, waits for them, and re-layouts  3.62 us (5%)
  between operations  3.3 us (4%)
  waiting for transfers between devices  3.04 us (4%)
  other arithmetic  2.94 us (4%)
    pallas_call x1, Pallas kernels, transform_fused(): pl.pallas_call(functools.partial(fused_kernel, pencils, bricks), out_shap...  53 us
    ppermute x2, starting transfers between devices, from_behind(): return lax.ppermute(block, axis, route)  6.56 us
    pallas_call x2, Pallas kernels, spread(): pl.pallas_call(functools.partial(spread_kernel, first_plane, coords.shape...  5.9 us
    unnamed x13, local copies, waits for them, and re-layouts  3.62 us
    ppermute x2, waiting for transfers between devices, from_behind(): return lax.ppermute(block, axis, route)  3.04 us
  transfers between devices with their start and end apart: 2, of which 1 were waited for; matrix products, arithmetic and copies ran while one was open for 0% of the time, Pallas kernels for 0%

profile of v3, /device:TPU:0, one launch (start us, length us, event | category | flops | bytes accessed | tf_op | source)
XLA Modules:
  0.0 78.3 jit_solution(2952630876530556908)
XLA Ops:
  0.6 0.0 copy-start.5
  0.6 0.0 copy-start.4
  0.7 0.0 copy-start
  0.7 0.0 copy-start.1
  1.5 0.7 pad_add_fusion.refs_0_
  2.2 0.7 fusion
  2.9 0.9 %pad_maximum_fusion.refs_1_ = f32[4,4096]{1,0:T(4,128)S(1)} fusion(f32[1,4096]{1,0:T(1,128)S(1)} %bitcast.3, f32[3,4096]{1,0:T(4,128)} %param.11), kind=kLoop, calls=%fused_computation | loop fusion | flops 16384 | bytes 131072 | tf_op jit(solution)/shard_map/concatenate | solution.py:449
  3.8 3.0 %shard_map.122.refs_2_ = f32[4,3,136,128]{3,2,1,0:T(8,128)S(1)} custom-call(s32[128]{0:T(128)S(1)} %pad_add_fusion.refs_0_, f32[4,4096]{1,0:T(4,128)S(1)} %pad_maximum_fusion.refs_1_), custom_call_target="tpu_custom_call" | custom-call | flops 20000000 | bytes 4000000 | tf_op jit(solution)/shard_map/pallas_call | solution.py:111
  6.8 6.1 %collective-permute-start.1 = (f32[4,4096]{1,0:T(4,128)S(1)}, f32[4,4096]{1,0:T(4,128)S(1)}, u32[]{:S(2)}, u32[]{:S(2)}) collective-permute-start(f32[4,4096]{1,0:T(4,128)S(1)} %pad_maximum_fusion.refs_1_), channel_id=1, source_target_pairs={{4,0},{8,4},{12,8},{16,12},{20,16},{24,20},{28,24},{0,28},{5,1},{9... | collective-permute-start | bytes 196616 | tf_op jit(solution)/shard_map/ppermute | solution.py:29
  12.8 0.5 collective-permute-start
  13.3 3.0 %collective-permute-done.refs_0_ = s32[128]{0:T(128)S(1)} collective-permute-done((s32[128]{0:T(128)S(1)}, s32[128]{0:T(128)S(1)}, u32[]{:S(2)}, u32[]{:S(2)}) %collective-permute-start) | collective-permute-done | bytes 544 | tf_op jit(solution)/shard_map/ppermute | solution.py:29
  16.4 0.0 collective-permute-done.1.refs_1_
  16.4 2.9 %shard_map.123.grid_ref = f32[4,3,136,128]{3,2,1,0:T(8,128)S(1)} custom-call(s32[128]{0:T(128)S(1)} %collective-permute-done.refs_0_, f32[4,4096]{1,0:T(4,128)S(1)} %collective-permute-done.1.refs_1_, f32[4,3,136,128]{3,2,1,0:T(8,128)S(1)} %shard_map.122.refs_2_), custom_call_target="tpu_custom_call" | custom-call | flops 20000000 | bytes 4000000 | tf_op jit(solution)/shard_map/pallas_call | solution.py:111
  19.3 0.0 copy-done.5
  19.3 0.0 copy-done.4
  19.4 0.0 copy-done
  19.4 0.0 copy-done.1
  19.4 0.0 copy-start.2
  19.4 1.2 %copy-done.2 = bf16[512,1024]{1,0:T(8,128)(2,1)S(1)} copy-done((bf16[512,1024]{1,0:T(8,128)(2,1)S(1)}, bf16[512,1024]{1,0:T(8,128)(2,1)}, u32[]{:S(2)}) %copy-start.2) | copy-done | bytes 1048600
  20.6 0.0 copy-start.3
  20.6 1.2 %copy-done.3 = bf16[512,1024]{1,0:T(8,128)(2,1)S(1)} copy-done((bf16[512,1024]{1,0:T(8,128)(2,1)S(1)}, bf16[512,1024]{1,0:T(8,128)(2,1)}, u32[]{:S(2)}) %copy-start.3) | copy-done | bytes 1048600
  21.8 53.0 %shard_map.124 = (f32[8,128]{1,0:T(8,128)S(1)}, f32[2,24,64,128]{3,2,1,0:T(8,128)S(1)}) custom-call(f32[4,3,136,128]{3,2,1,0:T(8,128)S(1)} %shard_map.123.grid_ref, bf16[512,1024]{1,0:T(8,128)(2,1)S(1)} %copy-done.3, bf16[512,1024]{1,0:T(8,128)(2,1)S(1)} %copy-done.2, bf16[1024,512]{1,0:T(8,128)(2,1)S(1)} %copy-done.1, bf16[1024,512]{1,0:T(8,128)(2,1)S(1)} %copy-done, ...), custom_call_target="tpu_custom_call" | custom-call | flops 6000000000 | bytes 8000000 | tf_op jit(solution)/shard_map/pallas_call | solution.py:409
  74.8 0.6 reduce_sum.9
  76.1 1.1 %copy.15 = f32[2,24,64,128]{3,2,1,0:T(8,128)} copy(f32[2,24,64,128]{3,2,1,0:T(8,128)S(1)} %get-tuple-element.15) | data formatting | bytes 3145728
Async XLA Ops:
  0.6 18.7 %copy-start.5 = (f32[2,8,512]{2,1,0:T(8,128)S(1)}, f32[2,8,512]{2,1,0:T(8,128)}, u32[]{:S(2)}) copy-start(f32[2,8,512]{2,1,0:T(8,128)} %constant.26.clone.xterm_ref) | copy-start | bytes 98308
  0.6 18.7 %copy-start.4 = (f32[2,512,128]{2,1,0:T(8,128)S(1)}, f32[2,512,128]{2,1,0:T(8,128)}, u32[]{:S(2)}) copy-start(f32[2,512,128]{2,1,0:T(8,128)} %constant.25.clone.yterm_any) | copy-start | bytes 1572868
  0.7 18.7 %copy-start = (bf16[1024,512]{1,0:T(8,128)(2,1)S(1)}, bf16[1024,512]{1,0:T(8,128)(2,1)}, u32[]{:S(2)}) copy-start(bf16[1024,512]{1,0:T(8,128)(2,1)} %constant.24.clone.ylow_any) | copy-start | bytes 3145732
  0.7 18.7 %copy-start.1 = (bf16[1024,512]{1,0:T(8,128)(2,1)S(1)}, bf16[1024,512]{1,0:T(8,128)(2,1)}, u32[]{:S(2)}) copy-start(bf16[1024,512]{1,0:T(8,128)(2,1)} %constant.23.clone.yhigh_any) | copy-start | bytes 3145732
  6.8 9.6 %collective-permute-start.1 = (f32[4,4096]{1,0:T(4,128)S(1)}, f32[4,4096]{1,0:T(4,128)S(1)}, u32[]{:S(2)}, u32[]{:S(2)}) collective-permute-start(f32[4,4096]{1,0:T(4,128)S(1)} %pad_maximum_fusion.refs_1_), channel_id=1, source_target_pairs={{4,0},{8,4},{12,8},{16,12},{20,16},{24,20},{28,24},{0,28},{5,1},{9... | collective-permute-start | bytes 196616 | tf_op jit(solution)/shard_map/ppermute | solution.py:29
  12.8 3.5 %collective-permute-start = (s32[128]{0:T(128)S(1)}, s32[128]{0:T(128)S(1)}, u32[]{:S(2)}, u32[]{:S(2)}) collective-permute-start(s32[128]{0:T(128)S(1)} %pad_add_fusion.refs_0_), channel_id=1, source_target_pairs={{4,0},{8,4},{12,8},{16,12},{20,16},{24,20},{28,24},{0,28},{5,1},{9... | collective-permute-start | bytes 1544 | tf_op jit(solution)/shard_map/ppermute | solution.py:29
  19.4 1.2 %copy-start.2 = (bf16[512,1024]{1,0:T(8,128)(2,1)S(1)}, bf16[512,1024]{1,0:T(8,128)(2,1)}, u32[]{:S(2)}) copy-start(bf16[512,1024]{1,0:T(8,128)(2,1)} %constant.22.clone.xlow_ref) | copy-start | bytes 3145732
  20.6 1.2 %copy-start.3 = (bf16[512,1024]{1,0:T(8,128)(2,1)S(1)}, bf16[512,1024]{1,0:T(8,128)(2,1)}, u32[]{:S(2)}) copy-start(bf16[512,1024]{1,0:T(8,128)(2,1)} %constant.21.clone.xhigh_ref) | copy-start | bytes 3145732

commit v4 on v3

--- a/solution.py
+++ b/solution.py
@@ -52,6 +52,7 @@
 def spread_kernel(first_plane, block_atoms, *refs):
     anchor_ref, coords_ref, *before, grid_ref = refs
     slots = anchor_ref.shape[0] // 2
+    count = anchor_ref[2 * slots]
     if before:
         grid_ref[...] = before[0][...]
     else:
@@ -66,7 +67,9 @@
 
     def turn(step, carry):
         here = pl.ds(pl.multiple_of(step * width, width), width)
-        depth = spline(coords_ref[0:1, here] - planes) * coords_ref[3:4, here]
+        live = lane_block[0:1] + step * GROUP < count
+        charge = jnp.where(live, coords_ref[3:4, here], 0.0)
+        depth = spline(coords_ref[0:1, here] - planes) * charge
         lines = spline(coords_ref[1:2, here] - steps)
         cells = split(spline(coords_ref[2:3, here] - steps))
         cells = [jnp.concatenate([part, blank], axis=0) for part in cells]
@@ -225,9 +228,9 @@
 
 def fused_kernel(
     pencils, bricks,
-    grid_ref, xhigh_ref, xlow_ref, yhigh_any, ylow_any, yterm_any, xterm_ref,
+    grid_ref, high_ref, low_ref, yterm_ref, xterm_ref,
     energy_ref, spectrum_ref,
-    yhigh_ref, ylow_ref, yterm_ref, fetched, xs, xr, ys, zr, ep, eb,
+    xs, xr, ys, zr, ep, eb,
     xsend, xrecv, zsend, zrecv, epsend, eprecv, ebsend, ebrecv,
 ):
     mine = {"pencil": lax.axis_index("pencil"), "brick": lax.axis_index("brick")}
@@ -257,14 +260,6 @@
             device_id={axis: peer(axis, step)}, device_id_type=pl.DeviceIdType.MESH,
         ).wait_recv()
 
-    fetches = [
-        pltpu.make_async_copy(source, target, fetched.at[i])
-        for i, (source, target) in enumerate(
-            [(yhigh_any, yhigh_ref), (ylow_any, ylow_ref), (yterm_any, yterm_ref)]
-        )
-    ]
-    for fetch in fetches:
-        fetch.start()
     barrier = pltpu.get_barrier_semaphore()
     for axis in sizes:
         for step in range(1, sizes[axis]):
@@ -284,10 +279,12 @@
 
     for plane in range(ZDEV):
         lines = jnp.concatenate([grid_ref[t, plane] for t in range(NX // LANES)], axis=1)
-        after_x = dot3(split(lines), (xhigh_ref[...], xlow_ref[...]), ((1,), (0,)))
-        width = after_x.shape[1] // pencils
+        lines = split(lines)
+        real = dot3(lines, (high_ref[0:NX], low_ref[0:NX]), ((1,), (0,)))
+        imag = -dot3(lines, (high_ref[NX:], low_ref[NX:]), ((1,), (0,)))
         for target in range(pencils):
-            xs[plane, target] = after_x[:, target * width : (target + 1) * width]
+            xs[plane, target, :, 0:LANES] = real[:, target * LANES : (target + 1) * LANES]
+            xs[plane, target, :, LANES:] = imag[:, target * LANES : (target + 1) * LANES]
         if plane == 0:
             pl.semaphore_wait(barrier, pencils + bricks - 2)
             send_lines(plane)
@@ -299,16 +296,13 @@
             arrived("pencil", step, xr.at[plane, other], xrecv.at[plane, other], xsend.at[plane, step])
         if plane + 1 < ZDEV:
             send_lines(plane + 1)
-        if plane == 0:
-            for fetch in fetches:
-                fetch.wait()
         pieces = []
         for source in range(pencils):
             pieces.append(xr[plane, source, RIM:rows])
             rim = xr[plane, (source + 1) % pencils, 0:RIM]
             pieces.append(xr[plane, source, rows : rows + RIM] + rim)
         columns = split(jnp.concatenate(pieces, axis=0))
-        both = dot3((yhigh_ref[...], ylow_ref[...]), columns, ((1,), (0,)))
+        both = dot3((high_ref[...], low_ref[...]), columns, ((1,), (0,)))
         real = both[:NY, :LANES] + both[NY:, LANES:]
         imag = both[:NY, LANES:] - both[NY:, :LANES]
         for target in range(bricks):
@@ -390,10 +384,6 @@
     pencils, bricks = lax.axis_size("pencil"), lax.axis_size("brick")
     part = NY // bricks
     columns = NX // pencils
-    cosine, sine = tables(NX)
-    turn_x = np.stack(
-        [cosine.reshape(NX, pencils, columns), -sine.reshape(NX, pencils, columns)], axis=2
-    ).reshape(NX, 2 * NX)
     cosine, sine = tables(NY)
     turn_y = np.concatenate([cosine, sine], axis=0)
 
@@ -412,13 +402,9 @@
             jax.ShapeDtypeStruct((8, LANES), f32),
             jax.ShapeDtypeStruct((2, ZDEV * bricks, part, columns), f32),
         ),
-        in_specs=[whole] * 3 + [pl.BlockSpec(memory_space=pl.ANY)] * 3 + [whole],
+        in_specs=[whole] * 5,
         out_specs=(whole, whole),
         scratch_shapes=[
-            pltpu.VMEM((2 * NY, NY), jnp.bfloat16),
-            pltpu.VMEM((2 * NY, NY), jnp.bfloat16),
-            pltpu.VMEM((2, NY, LANES), f32),
-            dma((3,)),
             pltpu.VMEM((ZDEV, pencils, rows + RIM, 2 * LANES), f32),
             pltpu.VMEM((ZDEV, pencils, rows + RIM, 2 * LANES), f32),
             pltpu.VMEM((ZDEV, bricks, part, 2 * LANES), f32),
@@ -435,23 +421,19 @@
         cost_estimate=pl.CostEstimate(
             flops=6_000_000_000, bytes_accessed=8_000_000, transcendentals=0
         ),
-    )(grid, *halves(turn_x), *halves(turn_y), y_terms.astype(np.float32), x_terms.astype(np.float32))
+    )(grid, *halves(turn_y), y_terms.astype(np.float32), x_terms.astype(np.float32))
     return jnp.sum(energy).reshape(1), spectrum
 
 
 def shards(positions, charges, anchor_row, anchor_column, counts):
     slot_count = anchor_row.shape[0]
     atoms = charges.shape[0]
-    block_atoms = atoms // slot_count
     rows = NY // lax.axis_size("pencil")
-    live = jnp.arange(atoms, dtype=jnp.int32) < counts[0] * block_atoms
-    charge = (charges * live.astype(jnp.float32)).reshape(1, atoms)
-    coords = jnp.concatenate([positions, charge], axis=0)
-    anchors = jnp.concatenate([anchor_row, anchor_column])
+    coords = jnp.concatenate([positions, charges.reshape(1, atoms)], axis=0)
+    anchors = jnp.concatenate([anchor_row, anchor_column, counts])
+    far_anchors, far_coords = (from_behind(array, "brick", -1) for array in (anchors, coords))
     grid = spread(3, rows, anchors, coords)
-    grid, anchors, coords = lax.optimization_barrier((grid, anchors, coords))
-    anchors, coords = (from_behind(array, "brick", -1) for array in (anchors, coords))
-    grid = spread(0, rows, anchors, coords, grid)
+    grid = spread(0, rows, far_anchors, far_coords, grid)
     bricks = lax.axis_size("brick")
     tiled = NX // lax.axis_size("pencil") == LANES and NY // bricks % 8 == 0
     if tiled and bricks & (bricks - 1) == 0:

time: 78.7 us -> 72 us (0.915)
  waiting for transfers between devices: 3.04 us -> 0.1 us
  local copies, waits for them, and re-layouts: 3.62 us -> 1.17 us
    ppermute x2, waiting for transfers between devices: 3.04 us -> 0.1 us  [from_behind(): return lax.ppermute(block, axis, route)]
    unnamed x13 -> x9, local copies, waits for them, and re-layouts: 3.62 us -> 1.17 us
  transfers between devices with their start and end apart: 2 -> 2, of which waited for: 1 -> 1; matrix products, arithmetic and copies ran while one was open for 0% -> 1% of each run, Pallas kernels for 0% -> 4%
where the time goes in v4:
time: 72 us; the launch traced here: 71.8 us
  Pallas kernels  58.5 us (81%)
  starting transfers between devices  6.56 us (9%)
  between operations  3.15 us (4%)
  other arithmetic  2.39 us (3%)
  local copies, waits for them, and re-layouts  1.17 us (2%)
    pallas_call x1, Pallas kernels, transform_fused(): pl.pallas_call(functools.partial(fused_kernel, pencils, bricks), out_shap...  52.5 us
    ppermute x2, starting transfers between devices, from_behind(): return lax.ppermute(block, axis, route)  6.56 us
    pallas_call x2, Pallas kernels, spread(): pl.pallas_call(functools.partial(spread_kernel, first_plane, coords.shape...  5.92 us
  transfers between devices with their start and end apart: 2, of which 1 were waited for; matrix products, arithmetic and copies ran while one was open for 1% of the time, Pallas kernels for 4%

profile of v4, /device:TPU:0, one launch (start us, length us, event | category | flops | bytes accessed | tf_op | source)
XLA Modules:
  0.0 71.8 jit_solution(9381839947362109324)
XLA Ops:
  0.6 0.0 copy-start.3
  0.6 0.0 copy-start.2
  0.7 0.0 copy-start
  0.7 0.0 copy-start.1
  0.7 1.0 %pad_maximum_fusion.refs_1_ = f32[4,4096]{1,0:T(4,128)S(1)} fusion(f32[1,4096]{1,0:T(1,128)} %bitcast.2, f32[3,4096]{1,0:T(4,128)} %param.9), kind=kLoop, calls=%fused_computation | loop fusion | flops 16384 | bytes 131072 | tf_op jit(solution)/shard_map/concatenate | solution.py:432
  1.7 6.1 %collective-permute-start.1 = (f32[4,4096]{1,0:T(4,128)S(1)}, f32[4,4096]{1,0:T(4,128)S(1)}, u32[]{:S(2)}, u32[]{:S(2)}) collective-permute-start(f32[4,4096]{1,0:T(4,128)S(1)} %pad_maximum_fusion.refs_1_), channel_id=1, source_target_pairs={{4,0},{8,4},{12,8},{16,12},{20,16},{24,20},{28,24},{0,28},{5,1},{9... | collective-permute-start | bytes 196616 | tf_op jit(solution)/shard_map/ppermute | solution.py:29
  8.4 0.8 %pad_add_fusion.refs_0_ = s32[129]{0:T(256)S(1)} fusion(s32[1]{0:T(128)S(6)} %copy.12, s32[64]{0:T(128)} %param.12, s32[64]{0:T(128)} %param.11), kind=kLoop, calls=%fused_computation.1 | loop fusion | flops 258 | bytes 1032 | tf_op jit(solution)/shard_map/concatenate | solution.py:433
  9.2 0.5 collective-permute-start
  9.7 3.0 %shard_map.104.refs_2_ = f32[4,3,136,128]{3,2,1,0:T(8,128)S(1)} custom-call(s32[129]{0:T(256)S(1)} %pad_add_fusion.refs_0_, f32[4,4096]{1,0:T(4,128)S(1)} %pad_maximum_fusion.refs_1_), custom_call_target="tpu_custom_call" | custom-call | flops 20000000 | bytes 4000000 | tf_op jit(solution)/shard_map/pallas_call | solution.py:114
  12.7 0.1 collective-permute-done.refs_0_
  12.8 0.0 collective-permute-done.1.refs_1_
  12.8 3.0 %shard_map.105.grid_ref = f32[4,3,136,128]{3,2,1,0:T(8,128)S(1)} custom-call(s32[129]{0:T(256)S(1)} %collective-permute-done.refs_0_, f32[4,4096]{1,0:T(4,128)S(1)} %collective-permute-done.1.refs_1_, f32[4,3,136,128]{3,2,1,0:T(8,128)S(1)} %shard_map.104.refs_2_), custom_call_target="tpu_custom_call" | custom-call | flops 20000000 | bytes 4000000 | tf_op jit(solution)/shard_map/pallas_call | solution.py:114
  15.7 0.0 copy-done.3
  15.7 0.0 copy-done.2
  15.7 0.0 copy-done
  15.8 0.0 copy-done.1
  15.8 52.5 %shard_map.106 = (f32[8,128]{1,0:T(8,128)S(1)}, f32[2,24,64,128]{3,2,1,0:T(8,128)S(1)}) custom-call(f32[4,3,136,128]{3,2,1,0:T(8,128)S(1)} %shard_map.105.grid_ref, bf16[1024,512]{1,0:T(8,128)(2,1)S(1)} %copy-done.1, bf16[1024,512]{1,0:T(8,128)(2,1)S(1)} %copy-done, f32[2,512,128]{2,1,0:T(8,128)S(1)} %copy-done.2, f32[2,8,512]{2,1,0:T(8,128)S(1)} %copy-done.3), custom_call_target="tpu_custom_call" | custom-call | flops 6000000000 | bytes 8000000 | tf_op jit(solution)/shard_map/pallas_call | solution.py:399
  68.3 0.6 reduce_sum.9
  69.6 1.1 %copy.13 = f32[2,24,64,128]{3,2,1,0:T(8,128)} copy(f32[2,24,64,128]{3,2,1,0:T(8,128)S(1)} %get-tuple-element.9) | data formatting | bytes 3145728
Async XLA Ops:
  0.6 15.1 %copy-start.3 = (f32[2,8,512]{2,1,0:T(8,128)S(1)}, f32[2,8,512]{2,1,0:T(8,128)}, u32[]{:S(2)}) copy-start(f32[2,8,512]{2,1,0:T(8,128)} %constant.16.clone.xterm_ref) | copy-start | bytes 98308
  0.6 15.1 %copy-start.2 = (f32[2,512,128]{2,1,0:T(8,128)S(1)}, f32[2,512,128]{2,1,0:T(8,128)}, u32[]{:S(2)}) copy-start(f32[2,512,128]{2,1,0:T(8,128)} %constant.15.clone.yterm_ref) | copy-start | bytes 1572868
  0.7 15.1 %copy-start = (bf16[1024,512]{1,0:T(8,128)(2,1)S(1)}, bf16[1024,512]{1,0:T(8,128)(2,1)}, u32[]{:S(2)}) copy-start(bf16[1024,512]{1,0:T(8,128)(2,1)} %constant.14.clone.low_ref) | copy-start | bytes 3145732
  0.7 15.1 %copy-start.1 = (bf16[1024,512]{1,0:T(8,128)(2,1)S(1)}, bf16[1024,512]{1,0:T(8,128)(2,1)}, u32[]{:S(2)}) copy-start(bf16[1024,512]{1,0:T(8,128)(2,1)} %constant.13.clone.high_ref) | copy-start | bytes 3145732
  1.7 11.0 %collective-permute-start.1 = (f32[4,4096]{1,0:T(4,128)S(1)}, f32[4,4096]{1,0:T(4,128)S(1)}, u32[]{:S(2)}, u32[]{:S(2)}) collective-permute-start(f32[4,4096]{1,0:T(4,128)S(1)} %pad_maximum_fusion.refs_1_), channel_id=1, source_target_pairs={{4,0},{8,4},{12,8},{16,12},{20,16},{24,20},{28,24},{0,28},{5,1},{9... | collective-permute-start | bytes 196616 | tf_op jit(solution)/shard_map/ppermute | solution.py:29
  9.2 3.6 %collective-permute-start = (s32[129]{0:T(256)S(1)}, s32[129]{0:T(256)S(1)}, u32[]{:S(2)}, u32[]{:S(2)}) collective-permute-start(s32[129]{0:T(256)S(1)} %pad_add_fusion.refs_0_), channel_id=1, source_target_pairs={{4,0},{8,4},{12,8},{16,12},{20,16},{24,20},{28,24},{0,28},{5,1},{9... | collective-permute-start | bytes 1556 | tf_op jit(solution)/shard_map/ppermute | solution.py:29

commit v5 on v4

--- a/solution.py
+++ b/solution.py
@@ -230,8 +230,8 @@
     pencils, bricks,
     grid_ref, high_ref, low_ref, yterm_ref, xterm_ref,
     energy_ref, spectrum_ref,
-    xs, xr, ys, zr, ep, eb,
-    xsend, xrecv, zsend, zrecv, epsend, eprecv, ebsend, ebrecv,
+    xs, xr, ys, zr, xs0, xr0, ys0, zr0, zd, ep, eb,
+    xsend, xrecv, zsend, zrecv, xsend0, xrecv0, zsend0, zrecv0, epsend, eprecv, ebsend, ebrecv,
 ):
     mine = {"pencil": lax.axis_index("pencil"), "brick": lax.axis_index("brick")}
     sizes = {"pencil": pencils, "brick": bricks}
@@ -270,6 +270,22 @@
 
     me, slab = mine["pencil"], mine["brick"]
 
+    half = LANES // 2
+
+    def send_first(part_index):
+        for step in range(1, pencils):
+            send(
+                "pencil", step, xs0.at[part_index, peer("pencil", step)], xr0.at[part_index, me],
+                xsend0.at[part_index, step], xrecv0.at[part_index, me],
+            )
+
+    def in_halves(real, imag):
+        low = lax.broadcasted_iota(jnp.int32, real.shape, 1) < half
+        return (
+            jnp.where(low, real, pltpu.roll(imag, half, 1)),
+            jnp.where(low, pltpu.roll(real, half, 1), imag),
+        )
+
     def send_lines(plane):
         for step in range(1, pencils):
             send(
@@ -282,26 +298,57 @@
         lines = split(lines)
         real = dot3(lines, (high_ref[0:NX], low_ref[0:NX]), ((1,), (0,)))
         imag = -dot3(lines, (high_ref[NX:], low_ref[NX:]), ((1,), (0,)))
+        if plane == 0:
+            for target in range(pencils):
+                own = slice(target * LANES, (target + 1) * LANES)
+                xs0[0, target], xs0[1, target] = in_halves(real[:, own], imag[:, own])
+            pl.semaphore_wait(barrier, pencils + bricks - 2)
+            send_first(0)
+            xr0[0, me] = xs0[0, me]
+            xr0[1, me] = xs0[1, me]
+            continue
         for target in range(pencils):
-            xs[plane, target, :, 0:LANES] = real[:, target * LANES : (target + 1) * LANES]
-            xs[plane, target, :, LANES:] = imag[:, target * LANES : (target + 1) * LANES]
-        if plane == 0:
-            pl.semaphore_wait(barrier, pencils + bricks - 2)
-            send_lines(plane)
-        xr[plane, me] = xs[plane, me]
-
-    for plane in range(ZDEV):
+            xs[plane - 1, target, :, 0:LANES] = real[:, target * LANES : (target + 1) * LANES]
+            xs[plane - 1, target, :, LANES:] = imag[:, target * LANES : (target + 1) * LANES]
+        xr[plane - 1, me] = xs[plane - 1, me]
+
+    def gathered(held):
+        pieces = []
+        for source in range(pencils):
+            pieces.append(held[source, RIM:rows])
+            pieces.append(held[source, rows : rows + RIM] + held[(source + 1) % pencils, 0:RIM])
+        return split(jnp.concatenate(pieces, axis=0))
+
+    for index in range(2):
+        for step in range(1, pencils):
+            other = peer("pencil", step)
+            arrived(
+                "pencil", step, xr0.at[index, other], xrecv0.at[index, other], xsend0.at[index, step]
+            )
+        if index == 0:
+            send_first(1)
+        else:
+            send_lines(0)
+        both = dot3((high_ref[...], low_ref[...]), gathered(xr0.at[index]), ((1,), (0,)))
+        turned = pltpu.roll(both[NY:], half, 1)
+        low = lax.broadcasted_iota(jnp.int32, turned.shape, 1) < half
+        both = both[:NY] + jnp.where(low, turned, -turned)
+        for target in range(bricks):
+            ys0[index, target] = both[target * part : (target + 1) * part]
+        for step in range(1, bricks):
+            send(
+                "brick", step, ys0.at[index, peer("brick", step)], zr0.at[index, slab],
+                zsend0.at[index, step], zrecv0.at[index, slab],
+            )
+        zr0[index, slab] = ys0[index, slab]
+
+    for plane in range(ZDEV - 1):
         for step in range(1, pencils):
             other = peer("pencil", step)
             arrived("pencil", step, xr.at[plane, other], xrecv.at[plane, other], xsend.at[plane, step])
-        if plane + 1 < ZDEV:
+        if plane + 1 < ZDEV - 1:
             send_lines(plane + 1)
-        pieces = []
-        for source in range(pencils):
-            pieces.append(xr[plane, source, RIM:rows])
-            rim = xr[plane, (source + 1) % pencils, 0:RIM]
-            pieces.append(xr[plane, source, rows : rows + RIM] + rim)
-        columns = split(jnp.concatenate(pieces, axis=0))
+        columns = gathered(xr.at[plane])
         both = dot3((high_ref[...], low_ref[...]), columns, ((1,), (0,)))
         real = both[:NY, :LANES] + both[NY:, LANES:]
         imag = both[:NY, LANES:] - both[NY:, :LANES]
@@ -317,19 +364,31 @@
 
     def over_bricks(plane, step, carry):
         here = pl.ds(pl.multiple_of(step * 8, 8), 8)
-        values = [
-            (zr[plane, b, here, 0:LANES], zr[plane, b, here, LANES : 2 * LANES])
-            for b in range(bricks)
-        ]
+        if plane == 0:
+            values = [in_halves(zr0[0, b, here, :], zr0[1, b, here, :]) for b in range(bricks)]
+        else:
+            values = [
+                (zr[0, b, here, 0:LANES], zr[0, b, here, LANES : 2 * LANES]) for b in range(bricks)
+            ]
         for k, (real, imag) in enumerate(radix_two(values)):
-            zr[plane, k, here, 0:LANES] = real
-            zr[plane, k, here, LANES : 2 * LANES] = imag
+            zd[plane, k, here, 0:LANES] = real
+            zd[plane, k, here, LANES : 2 * LANES] = imag
         return carry
 
-    for plane in range(ZDEV):
+    for index in range(2):
         for step in range(1, bricks):
             other = peer("brick", step)
-            arrived("brick", step, zr.at[plane, other], zrecv.at[plane, other], zsend.at[plane, step])
+            arrived(
+                "brick", step, zr0.at[index, other], zrecv0.at[index, other], zsend0.at[index, step]
+            )
+    for plane in range(ZDEV):
+        if plane > 0:
+            for step in range(1, bricks):
+                other = peer("brick", step)
+                arrived(
+                    "brick", step, zr.at[plane - 1, other], zrecv.at[plane - 1, other],
+                    zsend.at[plane - 1, step],
+                )
         if plane + 1 < ZDEV:
             lax.fori_loop(0, part // 8, functools.partial(over_bricks, plane), 0)
 
@@ -340,8 +399,8 @@
     def chunk(step, total):
         here = pl.ds(pl.multiple_of(step * 8, 8), 8)
         planes = [
-            [(zr[i, b, here, 0:LANES], zr[i, b, here, LANES : 2 * LANES]) for b in range(bricks)]
-            for i in range(ZDEV)
+            [(held[i, b, here, 0:LANES], held[i, b, here, LANES : 2 * LANES]) for b in range(bricks)]
+            for held, i in ((zd, 0), (zd, 1), (zr, 1))
         ]
         result = leading_transform(planes[:-1] + [radix_two(planes[-1])])
         across = pl.ds(pl.multiple_of(slab * part + step * 8, 8), 8)
@@ -405,14 +464,21 @@
         in_specs=[whole] * 5,
         out_specs=(whole, whole),
         scratch_shapes=[
-            pltpu.VMEM((ZDEV, pencils, rows + RIM, 2 * LANES), f32),
-            pltpu.VMEM((ZDEV, pencils, rows + RIM, 2 * LANES), f32),
-            pltpu.VMEM((ZDEV, bricks, part, 2 * LANES), f32),
-            pltpu.VMEM((ZDEV, bricks, part, 2 * LANES), f32),
+            pltpu.VMEM((ZDEV - 1, pencils, rows + RIM, 2 * LANES), f32),
+            pltpu.VMEM((ZDEV - 1, pencils, rows + RIM, 2 * LANES), f32),
+            pltpu.VMEM((ZDEV - 1, bricks, part, 2 * LANES), f32),
+            pltpu.VMEM((ZDEV - 1, bricks, part, 2 * LANES), f32),
+            pltpu.VMEM((2, pencils, rows + RIM, LANES), f32),
+            pltpu.VMEM((2, pencils, rows + RIM, LANES), f32),
+            pltpu.VMEM((2, bricks, part, LANES), f32),
+            pltpu.VMEM((2, bricks, part, LANES), f32),
+            pltpu.VMEM((2, bricks, part, 2 * LANES), f32),
             pltpu.VMEM((pencils, 8, LANES), f32),
             pltpu.VMEM((bricks, 8, LANES), f32),
             dma((ZDEV, pencils)), dma((ZDEV, pencils)),
             dma((ZDEV, bricks)), dma((ZDEV, bricks)),
+            dma((2, pencils)), dma((2, pencils)),
+            dma((2, bricks)), dma((2, bricks)),
             dma((pencils,)), dma((pencils,)), dma((bricks,)), dma((bricks,)),
         ],
         compiler_params=pltpu.CompilerParams(

time: 72 us -> 73.9 us (1.026)
  Pallas kernels: 58.5 us -> 60.3 us
    pallas_call x1, Pallas kernels: 52.5 us -> 54.4 us  [transform_fused(): pl.pallas_call(functools.partial(fused_kernel, pencils, bricks), out_shap...]
where the time goes in v5:
time: 73.9 us; the launch traced here: 73.7 us
  Pallas kernels  60.3 us (82%)
  starting transfers between devices  6.56 us (9%)
  between operations  3.15 us (4%)
  other arithmetic  2.39 us (3%)
  local copies, waits for them, and re-layouts  1.17 us (2%)
    pallas_call x1, Pallas kernels, transform_fused(): pl.pallas_call(functools.partial(fused_kernel, pencils, bricks), out_shap...  54.4 us
    ppermute x2, starting transfers between devices, from_behind(): return lax.ppermute(block, axis, route)  6.56 us
    pallas_call x2, Pallas kernels, spread(): pl.pallas_call(functools.partial(spread_kernel, first_plane, coords.shape...  5.91 us
  transfers between devices with their start and end apart: 2, of which 1 were waited for; matrix products, arithmetic and copies ran while one was open for 1% of the time, Pallas kernels for 4%

profile of v5, /device:TPU:0, one launch (start us, length us, event | category | flops | bytes accessed | tf_op | source)
XLA Modules:
  0.0 73.7 jit_solution(15645662491146339981)
XLA Ops:
  0.6 0.0 copy-start.3
  0.6 0.0 copy-start.2
  0.7 0.0 copy-start
  0.7 0.0 copy-start.1
  0.7 1.0 %pad_maximum_fusion.refs_1_ = f32[4,4096]{1,0:T(4,128)S(1)} fusion(f32[1,4096]{1,0:T(1,128)} %bitcast.2, f32[3,4096]{1,0:T(4,128)} %param.9), kind=kLoop, calls=%fused_computation | loop fusion | flops 16384 | bytes 131072 | tf_op jit(solution)/shard_map/concatenate | solution.py:498
  1.7 6.1 %collective-permute-start.1 = (f32[4,4096]{1,0:T(4,128)S(1)}, f32[4,4096]{1,0:T(4,128)S(1)}, u32[]{:S(2)}, u32[]{:S(2)}) collective-permute-start(f32[4,4096]{1,0:T(4,128)S(1)} %pad_maximum_fusion.refs_1_), channel_id=1, source_target_pairs={{4,0},{8,4},{12,8},{16,12},{20,16},{24,20},{28,24},{0,28},{5,1},{9... | collective-permute-start | bytes 196616 | tf_op jit(solution)/shard_map/ppermute | solution.py:29
  8.4 0.8 %pad_add_fusion.refs_0_ = s32[129]{0:T(256)S(1)} fusion(s32[1]{0:T(128)S(6)} %copy.12, s32[64]{0:T(128)} %param.12, s32[64]{0:T(128)} %param.11), kind=kLoop, calls=%fused_computation.1 | loop fusion | flops 258 | bytes 1032 | tf_op jit(solution)/shard_map/concatenate | solution.py:499
  9.2 0.5 collective-permute-start
  9.7 3.0 %shard_map.104.refs_2_ = f32[4,3,136,128]{3,2,1,0:T(8,128)S(1)} custom-call(s32[129]{0:T(256)S(1)} %pad_add_fusion.refs_0_, f32[4,4096]{1,0:T(4,128)S(1)} %pad_maximum_fusion.refs_1_), custom_call_target="tpu_custom_call" | custom-call | flops 20000000 | bytes 4000000 | tf_op jit(solution)/shard_map/pallas_call | solution.py:114
  12.7 0.1 collective-permute-done.refs_0_
  12.8 0.0 collective-permute-done.1.refs_1_
  12.8 3.0 %shard_map.105.grid_ref = f32[4,3,136,128]{3,2,1,0:T(8,128)S(1)} custom-call(s32[129]{0:T(256)S(1)} %collective-permute-done.refs_0_, f32[4,4096]{1,0:T(4,128)S(1)} %collective-permute-done.1.refs_1_, f32[4,3,136,128]{3,2,1,0:T(8,128)S(1)} %shard_map.104.refs_2_), custom_call_target="tpu_custom_call" | custom-call | flops 20000000 | bytes 4000000 | tf_op jit(solution)/shard_map/pallas_call | solution.py:114
  15.7 0.0 copy-done.3
  15.7 0.0 copy-done.2
  15.7 0.0 copy-done
  15.7 0.0 copy-done.1
  15.8 54.4 %shard_map.106 = (f32[8,128]{1,0:T(8,128)S(1)}, f32[2,24,64,128]{3,2,1,0:T(8,128)S(1)}) custom-call(f32[4,3,136,128]{3,2,1,0:T(8,128)S(1)} %shard_map.105.grid_ref, bf16[1024,512]{1,0:T(8,128)(2,1)S(1)} %copy-done.1, bf16[1024,512]{1,0:T(8,128)(2,1)S(1)} %copy-done, f32[2,512,128]{2,1,0:T(8,128)S(1)} %copy-done.2, f32[2,8,512]{2,1,0:T(8,128)S(1)} %copy-done.3), custom_call_target="tpu_custom_call" | custom-call | flops 6000000000 | bytes 8000000 | tf_op jit(solution)/shard_map/pallas_call | solution.py:458
  70.2 0.6 reduce_sum.9
  71.4 1.1 %copy.13 = f32[2,24,64,128]{3,2,1,0:T(8,128)} copy(f32[2,24,64,128]{3,2,1,0:T(8,128)S(1)} %get-tuple-element.9) | data formatting | bytes 3145728
Async XLA Ops:
  0.6 15.1 %copy-start.3 = (f32[2,8,512]{2,1,0:T(8,128)S(1)}, f32[2,8,512]{2,1,0:T(8,128)}, u32[]{:S(2)}) copy-start(f32[2,8,512]{2,1,0:T(8,128)} %constant.16.clone.xterm_ref) | copy-start | bytes 98308
  0.6 15.1 %copy-start.2 = (f32[2,512,128]{2,1,0:T(8,128)S(1)}, f32[2,512,128]{2,1,0:T(8,128)}, u32[]{:S(2)}) copy-start(f32[2,512,128]{2,1,0:T(8,128)} %constant.15.clone.yterm_ref) | copy-start | bytes 1572868
  0.7 15.1 %copy-start = (bf16[1024,512]{1,0:T(8,128)(2,1)S(1)}, bf16[1024,512]{1,0:T(8,128)(2,1)}, u32[]{:S(2)}) copy-start(bf16[1024,512]{1,0:T(8,128)(2,1)} %constant.14.clone.low_ref) | copy-start | bytes 3145732
  0.7 15.1 %copy-start.1 = (bf16[1024,512]{1,0:T(8,128)(2,1)S(1)}, bf16[1024,512]{1,0:T(8,128)(2,1)}, u32[]{:S(2)}) copy-start(bf16[1024,512]{1,0:T(8,128)(2,1)} %constant.13.clone.high_ref) | copy-start | bytes 3145732
  1.7 11.0 %collective-permute-start.1 = (f32[4,4096]{1,0:T(4,128)S(1)}, f32[4,4096]{1,0:T(4,128)S(1)}, u32[]{:S(2)}, u32[]{:S(2)}) collective-permute-start(f32[4,4096]{1,0:T(4,128)S(1)} %pad_maximum_fusion.refs_1_), channel_id=1, source_target_pairs={{4,0},{8,4},{12,8},{16,12},{20,16},{24,20},{28,24},{0,28},{5,1},{9... | collective-permute-start | bytes 196616 | tf_op jit(solution)/shard_map/ppermute | solution.py:29
  9.2 3.6 %collective-permute-start = (s32[129]{0:T(256)S(1)}, s32[129]{0:T(256)S(1)}, u32[]{:S(2)}, u32[]{:S(2)}) collective-permute-start(s32[129]{0:T(256)S(1)} %pad_add_fusion.refs_0_), channel_id=1, source_target_pairs={{4,0},{8,4},{12,8},{16,12},{20,16},{24,20},{28,24},{0,28},{5,1},{9... | collective-permute-start | bytes 1556 | tf_op jit(solution)/shard_map/ppermute | solution.py:29

commit v6 on v5

--- a/solution.py
+++ b/solution.py
@@ -304,6 +304,7 @@
                 xs0[0, target], xs0[1, target] = in_halves(real[:, own], imag[:, own])
             pl.semaphore_wait(barrier, pencils + bricks - 2)
             send_first(0)
+            send_first(1)
             xr0[0, me] = xs0[0, me]
             xr0[1, me] = xs0[1, me]
             continue
@@ -325,10 +326,7 @@
             arrived(
                 "pencil", step, xr0.at[index, other], xrecv0.at[index, other], xsend0.at[index, step]
             )
-        if index == 0:
-            send_first(1)
-        else:
-            send_lines(0)
+        send_lines(index)
         both = dot3((high_ref[...], low_ref[...]), gathered(xr0.at[index]), ((1,), (0,)))
         turned = pltpu.roll(both[NY:], half, 1)
         low = lax.broadcasted_iota(jnp.int32, turned.shape, 1) < half
@@ -346,8 +344,6 @@
         for step in range(1, pencils):
             other = peer("pencil", step)
             arrived("pencil", step, xr.at[plane, other], xrecv.at[plane, other], xsend.at[plane, step])
-        if plane + 1 < ZDEV - 1:
-            send_lines(plane + 1)
         columns = gathered(xr.at[plane])
         both = dot3((high_ref[...], low_ref[...]), columns, ((1,), (0,)))
         real = both[:NY, :LANES] + both[NY:, LANES:]

time: 73.9 us -> 73.5 us (level)
  no operation moved by 1% of the time
where the time goes in v6:
time: 73.5 us; the launch traced here: 73.3 us
  Pallas kernels  59.9 us (81%)
  starting transfers between devices  6.56 us (9%)
  between operations  3.15 us (4%)
  other arithmetic  2.39 us (3%)
  local copies, waits for them, and re-layouts  1.17 us (2%)
    pallas_call x1, Pallas kernels, transform_fused(): pl.pallas_call(functools.partial(fused_kernel, pencils, bricks), out_shap...  54 us
    ppermute x2, starting transfers between devices, from_behind(): return lax.ppermute(block, axis, route)  6.56 us
    pallas_call x2, Pallas kernels, spread(): pl.pallas_call(functools.partial(spread_kernel, first_plane, coords.shape...  5.92 us
  transfers between devices with their start and end apart: 2, of which 1 were waited for; matrix products, arithmetic and copies ran while one was open for 1% of the time, Pallas kernels for 4%

profile of v6, /device:TPU:0, one launch (start us, length us, event | category | flops | bytes accessed | tf_op | source)
XLA Modules:
  0.0 73.3 jit_solution(3657913103063258934)
XLA Ops:
  0.6 0.0 copy-start.3
  0.6 0.0 copy-start.2
  0.7 0.0 copy-start
  0.7 0.0 copy-start.1
  0.7 1.0 %pad_maximum_fusion.refs_1_ = f32[4,4096]{1,0:T(4,128)S(1)} fusion(f32[1,4096]{1,0:T(1,128)} %bitcast.2, f32[3,4096]{1,0:T(4,128)} %param.9), kind=kLoop, calls=%fused_computation | loop fusion | flops 16384 | bytes 131072 | tf_op jit(solution)/shard_map/concatenate | solution.py:494
  1.7 6.1 %collective-permute-start.1 = (f32[4,4096]{1,0:T(4,128)S(1)}, f32[4,4096]{1,0:T(4,128)S(1)}, u32[]{:S(2)}, u32[]{:S(2)}) collective-permute-start(f32[4,4096]{1,0:T(4,128)S(1)} %pad_maximum_fusion.refs_1_), channel_id=1, source_target_pairs={{4,0},{8,4},{12,8},{16,12},{20,16},{24,20},{28,24},{0,28},{5,1},{9... | collective-permute-start | bytes 196616 | tf_op jit(solution)/shard_map/ppermute | solution.py:29
  8.4 0.8 %pad_add_fusion.refs_0_ = s32[129]{0:T(256)S(1)} fusion(s32[1]{0:T(128)S(6)} %copy.12, s32[64]{0:T(128)} %param.12, s32[64]{0:T(128)} %param.11), kind=kLoop, calls=%fused_computation.1 | loop fusion | flops 258 | bytes 1032 | tf_op jit(solution)/shard_map/concatenate | solution.py:495
  9.2 0.5 collective-permute-start
  9.7 3.0 %shard_map.104.refs_2_ = f32[4,3,136,128]{3,2,1,0:T(8,128)S(1)} custom-call(s32[129]{0:T(256)S(1)} %pad_add_fusion.refs_0_, f32[4,4096]{1,0:T(4,128)S(1)} %pad_maximum_fusion.refs_1_), custom_call_target="tpu_custom_call" | custom-call | flops 20000000 | bytes 4000000 | tf_op jit(solution)/shard_map/pallas_call | solution.py:114
  12.7 0.1 collective-permute-done.refs_0_
  12.8 0.0 collective-permute-done.1.refs_1_
  12.8 3.0 %shard_map.105.grid_ref = f32[4,3,136,128]{3,2,1,0:T(8,128)S(1)} custom-call(s32[129]{0:T(256)S(1)} %collective-permute-done.refs_0_, f32[4,4096]{1,0:T(4,128)S(1)} %collective-permute-done.1.refs_1_, f32[4,3,136,128]{3,2,1,0:T(8,128)S(1)} %shard_map.104.refs_2_), custom_call_target="tpu_custom_call" | custom-call | flops 20000000 | bytes 4000000 | tf_op jit(solution)/shard_map/pallas_call | solution.py:114
  15.7 0.0 copy-done.3
  15.7 0.0 copy-done.2
  15.7 0.0 copy-done
  15.7 0.0 copy-done.1
  15.8 54.0 %shard_map.106 = (f32[8,128]{1,0:T(8,128)S(1)}, f32[2,24,64,128]{3,2,1,0:T(8,128)S(1)}) custom-call(f32[4,3,136,128]{3,2,1,0:T(8,128)S(1)} %shard_map.105.grid_ref, bf16[1024,512]{1,0:T(8,128)(2,1)S(1)} %copy-done.1, bf16[1024,512]{1,0:T(8,128)(2,1)S(1)} %copy-done, f32[2,512,128]{2,1,0:T(8,128)S(1)} %copy-done.2, f32[2,8,512]{2,1,0:T(8,128)S(1)} %copy-done.3), custom_call_target="tpu_custom_call" | custom-call | flops 6000000000 | bytes 8000000 | tf_op jit(solution)/shard_map/pallas_call | solution.py:454
  69.8 0.6 reduce_sum.9
  71.0 1.1 %copy.13 = f32[2,24,64,128]{3,2,1,0:T(8,128)} copy(f32[2,24,64,128]{3,2,1,0:T(8,128)S(1)} %get-tuple-element.9) | data formatting | bytes 3145728
Async XLA Ops:
  0.6 15.1 %copy-start.3 = (f32[2,8,512]{2,1,0:T(8,128)S(1)}, f32[2,8,512]{2,1,0:T(8,128)}, u32[]{:S(2)}) copy-start(f32[2,8,512]{2,1,0:T(8,128)} %constant.16.clone.xterm_ref) | copy-start | bytes 98308
  0.6 15.1 %copy-start.2 = (f32[2,512,128]{2,1,0:T(8,128)S(1)}, f32[2,512,128]{2,1,0:T(8,128)}, u32[]{:S(2)}) copy-start(f32[2,512,128]{2,1,0:T(8,128)} %constant.15.clone.yterm_ref) | copy-start | bytes 1572868
  0.7 15.1 %copy-start = (bf16[1024,512]{1,0:T(8,128)(2,1)S(1)}, bf16[1024,512]{1,0:T(8,128)(2,1)}, u32[]{:S(2)}) copy-start(bf16[1024,512]{1,0:T(8,128)(2,1)} %constant.14.clone.low_ref) | copy-start | bytes 3145732
  0.7 15.1 %copy-start.1 = (bf16[1024,512]{1,0:T(8,128)(2,1)S(1)}, bf16[1024,512]{1,0:T(8,128)(2,1)}, u32[]{:S(2)}) copy-start(bf16[1024,512]{1,0:T(8,128)(2,1)} %constant.13.clone.high_ref) | copy-start | bytes 3145732
  1.7 11.0 %collective-permute-start.1 = (f32[4,4096]{1,0:T(4,128)S(1)}, f32[4,4096]{1,0:T(4,128)S(1)}, u32[]{:S(2)}, u32[]{:S(2)}) collective-permute-start(f32[4,4096]{1,0:T(4,128)S(1)} %pad_maximum_fusion.refs_1_), channel_id=1, source_target_pairs={{4,0},{8,4},{12,8},{16,12},{20,16},{24,20},{28,24},{0,28},{5,1},{9... | collective-permute-start | bytes 196616 | tf_op jit(solution)/shard_map/ppermute | solution.py:29
  9.2 3.6 %collective-permute-start = (s32[129]{0:T(256)S(1)}, s32[129]{0:T(256)S(1)}, u32[]{:S(2)}, u32[]{:S(2)}) collective-permute-start(s32[129]{0:T(256)S(1)} %pad_add_fusion.refs_0_), channel_id=1, source_target_pairs={{4,0},{8,4},{12,8},{16,12},{20,16},{24,20},{28,24},{0,28},{5,1},{9... | collective-permute-start | bytes 1556 | tf_op jit(solution)/shard_map/ppermute | solution.py:29
